TPU v7x, 256 devices: a whole 4x4x8 slice. The times are simulated.
256 devices in a mesh: ctx: 8 (over y_lo, x), tp: 32 (over y_hi, z, core).
Axes of the slice: x: 4, y: 4 (y_hi: 2, y_lo: 2; y = y_hi * 2 + y_lo), z: 8, core: 2. Of those that a mesh axis runs over, the one named last changes fastest.
Arguments:
- hidden: bfloat16 [4096, 4096], P('ctx'), may hold values from -6 to 6
- mask_flags: int32 [4096], P('ctx'), may hold values 0 or 1
- mask_embed: bfloat16 [4096], replicated, may hold values from -6 to 6
- norm_gain: float32 [4096], replicated, may hold values from 0.1 to 1.9
- w_query: bfloat16 [4096, 4096], P(None, 'tp')
- w_key: bfloat16 [4096, 4096], P(None, 'tp')
- w_value: bfloat16 [4096, 4096], P(None, 'tp'), may hold values from -0.09375 to 0.09375
- w_out: bfloat16 [4096, 4096], P('tp'), may hold values from -0.5 to 0.5
Outputs:
- attended: bfloat16 [4096, 4096], P('ctx', 'tp')
All inputs are finite; a program needn't handle non-finite values. No bound on the sum of `mask_flags` on one device may be relied on, other than what follows from the above.
Results may differ from a plain program's by a relative error of at most 0.017.
Values may be sent and summed in bfloat16 or wider, within the bound.
A program may use at most 64 MiB of HBM per device.

v0:
```python
import math

import jax
import jax.numpy as jnp
from jax import lax
from jax.sharding import PartitionSpec as P

HD = 128


def rotate(block, angles):
    half = block.shape[-1] // 2
    first = block[..., :half]
    second = block[..., half:]
    cosine = jnp.cos(angles)[:, None, :]
    sine = jnp.sin(angles)[:, None, :]
    return jnp.concatenate(
        [first * cosine - second * sine, second * cosine + first * sine], axis=-1
    )


def on_device(hidden, mask_flags, mask_embed, norm_gain, w_query, w_key, w_value, w_out):
    rows = hidden.shape[0]
    head_dim = HD
    group_width = w_query.shape[1]
    local_heads = group_width // head_dim
    tokens = jnp.where(mask_flags[:, None] == 1, mask_embed[None, :], hidden)
    floats = tokens.astype(jnp.float32)
    scale_rows = lax.rsqrt(jnp.mean(floats * floats, axis=1, keepdims=True) + 1e-05)
    normed = (floats * scale_rows * norm_gain[None, :]).astype(jnp.bfloat16)
    start_row = lax.axis_index("ctx") * rows
    positions = (start_row + jnp.arange(rows)).astype(jnp.float32)
    freqs = jnp.power(500000.0, -2.0 * jnp.arange(head_dim // 2).astype(jnp.float32) / head_dim)
    angles = positions[:, None] * freqs[None, :]
    queries = jnp.dot(normed, w_query, preferred_element_type=jnp.float32).reshape(
        rows, local_heads, head_dim
    )
    keys = jnp.dot(normed, w_key, preferred_element_type=jnp.float32).reshape(
        rows, local_heads, head_dim
    )
    queries = rotate(queries, angles).astype(jnp.bfloat16)
    keys = rotate(keys, angles).astype(jnp.bfloat16)
    values = (
        jnp.dot(normed, w_value, preferred_element_type=jnp.float32)
        .astype(jnp.bfloat16)
        .reshape(rows, local_heads, head_dim)
    )
    inverse_root = 1.0 / math.sqrt(head_dim)
    running_top = jnp.full((local_heads, rows), -1e30, jnp.float32)
    piece_keys = lax.all_gather(keys, "ctx", axis=0, tiled=True)
    piece_values = lax.all_gather(values, "ctx", axis=0, tiled=True)
    scores = (
        jnp.einsum("qhd,khd->hqk", queries, piece_keys, preferred_element_type=jnp.float32)
        * inverse_root
    )
    new_top = jnp.maximum(running_top, jnp.max(scores, axis=2))
    exps = jnp.exp(scores - new_top[:, :, None])
    new_sum = jnp.sum(exps, axis=2)
    weights = exps.astype(jnp.bfloat16)
    added = jnp.einsum("hqk,khd->hqd", weights, piece_values, preferred_element_type=jnp.float32)
    mixed = (added / new_sum[:, :, None]).astype(jnp.bfloat16)
    mixed = jnp.transpose(mixed, (1, 0, 2)).reshape(rows, group_width)
    terms = jnp.dot(mixed, w_out, preferred_element_type=jnp.float32)
    result = lax.psum_scatter(terms.astype(jnp.bfloat16), "tp", scatter_dimension=1, tiled=True)
    return result


def solution(mesh):
    in_specs = (
        P("ctx", None),
        P("ctx"),
        P(),
        P(),
        P(None, "tp"),
        P(None, "tp"),
        P(None, "tp"),
        P("tp", None),
    )
    out_specs = P("ctx", "tp")
    return jax.shard_map(
        on_device, mesh=mesh, in_specs=in_specs, out_specs=out_specs, check_vma=False
    )
```

profile of v0, /device:TPU:6, one launch (start us, length us, event | category | flops | bytes accessed | tf_op | source)
XLA Modules:
  0.0 258.3 jit_solution(14690953615393795284)
XLA Ops:
  6.5 0.0 copy-start
  6.5 0.0 copy-start.3
  6.5 0.0 all-gather.4.cloned.1.call-start
  6.6 0.8 broadcast_compare_fusion
  7.4 3.4 %fusion = f32[512]{0:T(512)S(1)} fusion(bf16[512,4096]{1,0:T(8,128)(2,1)} %param.8, bf16[4096]{0:T(1024)(128)(2,1)} %param.10, pred[512]{0:T(512)(128)(4,1)S(1)} %broadcast_compare_fusion), kind=kLoop, calls=%fused_computation.2 | loop fusion | flops 8388096 | bytes 4205056 | tf_op jit(solution)/shard_map/reduce_sum | solution.py:29
  10.8 0.0 copy-start.4
  10.8 3.8 %fusion.2 = bf16[512,4096]{1,0:T(8,128)(2,1)S(1)} fusion(f32[4096]{0:T(1024)} %param.11, f32[512]{0:T(512)S(1)} %add_rsqrt_fusion, bf16[512,4096]{1,0:T(8,128)(2,1)} %param.8, bf16[4096]{0:T(1024)(128)(2,1)} %param.10, pred[512]{0:T(512)(128)(4,1)S(1)} %broadcast_compare_fusion), kind=kLoop, calls=%fused_computation.4 | loop fusion | flops 10485760 | bytes 8415744 | tf_op jit(solution)/shard_map/convert_element_type | solution.py:30
  14.7 0.0 copy-done.3
  14.7 0.0 copy-start.2
  14.7 0.0 copy-start.5
  14.7 1.5 convolution_bitcast_fusion
  16.2 0.4 copy-done.2
  16.6 0.0 copy-done.4
  16.6 1.5 convolution_bitcast_fusion.1
  18.1 0.6 fusion.38
  18.7 0.7 pad_maximum_fusion
  19.4 0.0 all-gather.4.cloned.1.call-update
  19.4 0.0 all-gather.6.cloned.1.call-start
  19.5 0.0 copy-done.5
  19.5 4.1 %convolution_convert_fusion.1 = bf16[512,128]{1,0:T(8,128)(2,1)} fusion(bf16[512,4096]{1,0:T(8,128)(2,1)} %copy-done.2, bf16[4096,128]{1,0:T(8,128)(2,1)S(1)} %copy-done.5), kind=kOutput, calls=%fused_computation.14 | convolution fusion | flops 536936448 | bytes 5373952 | tf_op jit(solution)/shard_map/dot_general | solution.py:44
  23.6 0.0 all-gather.6.cloned.1.call-update
  23.6 0.2 reduce-scatter.4.cloned.1.call-start
  23.8 38.1 %all-gather.4.cloned.1.call-done = bf16[4096,1,128]{0,2,1:T(8,128)(2,1)} async-done(((bf16[512,1,128]{0,2,1:T(8,128)(2,1)}), bf16[4096,1,128]{0,2,1:T(8,128)(2,1)}) %all-gather.4.cloned.1.call-update) | async-done | bytes 1048592 | tf_op jit(solution)/shard_map/all_gather | solution.py:50
  61.9 2.6 %multiply_reduce_fusion = (f32[512]{0:T(512)S(1)}, f32[512,4096]{1,0:T(8,128)S(1)}) fusion(bf16[4096,1,128]{0,2,1:T(8,128)(2,1)} %all-gather.4.cloned.1.call-done, bf16[512,64]{0,1:T(8,128)(2,1)S(1)} %get-tuple-element.6, bf16[512,64]{0,1:T(8,128)(2,1)S(1)} %get-tuple-element.5), kind=kOutput, calls=%fused_computation.6 | convolution fusion | flops 541326848 | bytes 9570304 | tf_op jit(solution)/shard_map/qhd,khd->hqk/dot_general | solution.py:53
  64.5 0.0 copy-start.1
  64.5 3.2 %copy-done.1 = f32[512,4096]{1,0:T(8,128)} copy-done((f32[512,4096]{1,0:T(8,128)}, f32[512,4096]{1,0:T(8,128)S(1)}, u32[]{:S(2)}) %copy-start.1) | copy-done | bytes 8388632
  67.7 1.5 fusion.3
  69.2 35.2 %all-gather.6.cloned.1.call-done = bf16[4096,128]{1,0:T(8,128)(2,1)} async-done(((bf16[512,128]{1,0:T(8,128)(2,1)}), bf16[4096,128]{1,0:T(8,128)(2,1)}) %all-gather.6.cloned.1.call-update) | async-done | bytes 1048592 | tf_op jit(solution)/shard_map/all_gather | solution.py:51
  104.4 0.0 copy-done
  104.4 10.1 %convolution_convert_fusion = bf16[512,4096]{1,0:T(8,128)(2,1)} fusion(bf16[128,4096]{1,0:T(8,128)(2,1)S(1)} %copy-done, bf16[4096,128]{1,0:T(8,128)(2,1)} %all-gather.6.cloned.1.call-done, f32[512,4096]{1,0:T(8,128)} %copy-done.1, f32[512]{0:T(512)S(1)} %broadcast_maximum_fusion, f32[512]{0:T(512)S(1)} %fusion.3), kind=kOutput, calls=%fused_computation.9 | convolution fusion | flops 1082261504 | bytes 14684160 | tf_op jit(solution)/shard_map/dot_general | solution.py:63
  114.5 6.5 %copy.9 = bf16[512,4096]{0,1:T(8,128)(2,1)} copy(bf16[512,4096]{1,0:T(8,128)(2,1)} %convolution_convert_fusion) | data formatting | bytes 8388608
  121.0 0.0 reduce-scatter.4.cloned.1.call-update
  121.0 129.1 %reduce-scatter.4.cloned.1.call-done = bf16[128,512]{1,0:T(8,128)(2,1)} async-done(((bf16[4096,512]{1,0:T(8,128)(2,1)}), bf16[128,512]{1,0:T(8,128)(2,1)}) %reduce-scatter.4.cloned.1.call-update) | async-done | bytes 131088
  250.1 1.7 copy.10
  (4 shorter events, 0.0 us)
Async XLA Ops:
  6.5 97.9 %copy-start = (bf16[128,4096]{1,0:T(8,128)(2,1)S(1)}, bf16[128,4096]{1,0:T(8,128)(2,1)}, u32[]{:S(2)}) copy-start(bf16[128,4096]{1,0:T(8,128)(2,1)} %param.15) | copy-start | bytes 3145732
  6.5 8.1 %copy-start.3 = (bf16[4096,128]{1,0:T(8,128)(2,1)S(1)}, bf16[4096,128]{1,0:T(8,128)(2,1)}, u32[]{:S(2)}) copy-start(bf16[4096,128]{1,0:T(8,128)(2,1)} %param.13) | copy-start | bytes 3145732
  6.5 55.3 %all-gather.4.cloned.1.call-start = ((), (), s32[]{:S(2)}) async-start(), calls=%async_computation.1 | async-start | bytes 1179648 | tf_op jit(solution)/shard_map/all_gather | solution.py:50
  10.8 5.8 %copy-start.4 = (bf16[4096,128]{1,0:T(8,128)(2,1)S(1)}, bf16[4096,128]{1,0:T(8,128)(2,1)}, u32[]{:S(2)}) copy-start(bf16[4096,128]{1,0:T(8,128)(2,1)} %param.12) | copy-start | bytes 3145732
  14.7 1.9 copy-start.2
  14.7 4.8 %copy-start.5 = (bf16[4096,128]{1,0:T(8,128)(2,1)S(1)}, bf16[4096,128]{1,0:T(8,128)(2,1)}, u32[]{:S(2)}) copy-start(bf16[4096,128]{1,0:T(8,128)(2,1)} %param.14) | copy-start | bytes 3145732
  19.4 85.0 %all-gather.6.cloned.1.call-start = ((), (), s32[]{:S(2)}) async-start(), calls=%async_computation.2 | async-start | bytes 1179648 | tf_op jit(solution)/shard_map/all_gather | solution.py:51
  23.6 226.5 %reduce-scatter.4.cloned.1.call-start = ((), (), s32[]{:S(2)}) async-start(), calls=%async_computation.3 | async-start | bytes 4325376
  64.5 3.2 %copy-start.1 = (f32[512,4096]{1,0:T(8,128)}, f32[512,4096]{1,0:T(8,128)S(1)}, u32[]{:S(2)}) copy-start(f32[512,4096]{1,0:T(8,128)S(1)} %get-tuple-element.12) | copy-start | bytes 25165828
Sparse Core Ops, SparseCore 0:
  19.5 42.3 all-gather.3
  63.7 40.6 all-gather.5
  121.1 128.9 reduce-scatter.3
where the time goes:
time: 259 us; the launch traced here: 258 us
  waiting for transfers between devices  202 us (78%)
  matrix products  19.8 us (8%)
  between operations  13.2 us (5%)
  local copies, waits for them, and re-layouts  11.8 us (5%)
  other arithmetic  10.8 us (4%)
    unnamed x4, waiting for transfers between devices  129 us
    all_gather x1, waiting for transfers between devices, on_device(): piece_keys = lax.all_gather(keys, 'ctx', axis=0, tiled=True)  38.1 us
    all_gather x1, waiting for transfers between devices, on_device(): piece_values = lax.all_gather(values, 'ctx', axis=0, tiled=True)  35.2 us
    unnamed x14, local copies, waits for them, and re-layouts  11.8 us
    dot_general x1, matrix products, on_device(): terms = jnp.dot(mixed, w_out, preferred_element_type=jnp.float32)  10.1 us
  transfers between devices with their start and end apart: 3, of which 3 were waited for; matrix products, arithmetic and copies ran while one was open for 3% of the time, Pallas kernels for 0%

commit v1 on v0

v1 whole, which is shorter than its diff:
```python
import math

import numpy as np
import jax
import jax.numpy as jnp
from jax import lax
from jax.sharding import PartitionSpec as P
from jax.experimental import pallas as pl
from jax.experimental.pallas import tpu as pltpu

D = 4096
HD = 128
SEQ = 4096
ROWS = 512
XROWS = 528
KB = 512
NKB = D // KB
R = 4
RB = ROWS // R
QB = 256
NZ = 8
NX = 4
MESH = pl.DeviceIdType.MESH
F32 = jnp.float32
BF16 = jnp.bfloat16


def rope_table():
    freqs = 500000.0 ** (-2.0 * np.arange(HD // 2) / HD)
    angles = np.arange(SEQ)[:, None] * freqs[None, :]
    return np.concatenate([np.cos(angles), np.sin(angles)], axis=1).astype(np.float32)


def kernel(hid, mask, emb, gain, wq, wk, wv, wo, tab, out,
           x, wkv_s, wq_s, emb_s, gain_s, mask_s, tab_s, maskc, ss, acc, qacc,
           kv, qs, m_s, o_s, mixed, mbuf, wd, part, rb, sb,
           ld_x, ld_k, ld_v, ld_s, ld_w, w_send, w_recv, sw_send, sw_recv,
           kv_send, kv_recv, m_send, m_recv, z_send, z_recv):
    ctx = lax.axis_index("ctx")
    tp = lax.axis_index("tp")
    xi, ylo = lax.rem(ctx, NX), lax.div(ctx, NX)
    yhi, z, core = lax.div(tp, 16), lax.rem(lax.div(tp, 2), NZ), lax.rem(tp, 2)
    diag = core == ylo
    off = core != ylo

    def dev(x_=xi, ylo_=ylo, yhi_=yhi, z_=z, core_=core):
        return (ylo_ * NX + x_, yhi_ * 16 + z_ * 2 + core_)

    xr, xl = lax.rem(xi + 1, NX), lax.rem(xi + NX - 1, NX)
    xo = lax.rem(xi + 2, NX)
    zr, zl = lax.rem(z + 1, NZ), lax.rem(z + NZ - 1, NZ)
    oc, oylo, oyhi = 1 - core, 1 - ylo, 1 - yhi

    loads = []
    c_gain = pltpu.make_async_copy(gain, gain_s, ld_s.at[0])
    c_emb = pltpu.make_async_copy(emb, emb_s, ld_s.at[1])
    c_mask = pltpu.make_async_copy(mask, mask_s, ld_s.at[2])
    c_tab = pltpu.make_async_copy(
        tab.at[pl.ds(pl.multiple_of(ctx * ROWS, ROWS), ROWS)], tab_s, ld_s.at[3])
    c_wq = pltpu.make_async_copy(wq, wq_s, ld_s.at[4])
    c_emb.start()
    c_gain.start()

    def xcopies(k):
        cols = pl.ds(pl.multiple_of(k * KB, KB), KB)
        return (
            pltpu.make_async_copy(hid.at[:, cols], x.at[pl.ds(0, ROWS), cols], ld_x.at[k]),
            pltpu.make_async_copy(wk.at[cols], wkv_s.at[cols, pl.ds(0, HD)], ld_k.at[k]),
            pltpu.make_async_copy(wv.at[cols], wkv_s.at[cols, pl.ds(HD, HD)], ld_v.at[k]),
        )

    def start_loads(k, _):
        for c in xcopies(k):
            c.start()
        return 0

    lax.fori_loop(0, NKB, start_loads, 0)
    c_mask.start()
    c_tab.start()
    c_wq.start()

    barrier = pltpu.get_barrier_semaphore()
    partners = [dev(x_=xr), dev(x_=xl), dev(z_=zr), dev(z_=zl), dev(core_=oc)]
    for c in (0, 1):
        partners += [dev(ylo_=oylo, core_=c), dev(yhi_=oyhi, core_=c),
                     dev(ylo_=oylo, yhi_=oyhi, core_=c)]
    for p in partners:
        pl.semaphore_signal(barrier, inc=1, device_id=p, device_id_type=MESH)
    pl.semaphore_wait(barrier, len(partners))

    my_rows = pl.ds(pl.multiple_of((yhi * 2 + core) * HD, HD), HD)

    def wsrc(half, zz, c):
        return wo.at[:, pl.ds(pl.multiple_of(half * 2048 + zz * 256 + c * HD, HD), HD)]

    def wdst(zz):
        return wd.at[my_rows, pl.ds(pl.multiple_of(zz * HD, HD), HD)]

    def wcopies(zz):
        return (
            pltpu.make_async_copy(wsrc(yhi, zz, core), wdst(zz), ld_w.at[0]),
            pltpu.make_async_remote_copy(
                wsrc(yhi, zz, oc), wdst(zz), w_send.at[0], w_recv.at[0],
                device_id=dev(core_=oc), device_id_type=MESH),
            pltpu.make_async_remote_copy(
                wsrc(oyhi, zz, 0), wdst(zz), w_send.at[1], w_recv.at[1 + core],
                device_id=dev(ylo_=oylo, yhi_=oyhi, core_=0), device_id_type=MESH),
            pltpu.make_async_remote_copy(
                wsrc(oyhi, zz, 1), wdst(zz), w_send.at[2], w_recv.at[1 + core],
                device_id=dev(ylo_=oylo, yhi_=oyhi, core_=1), device_id_type=MESH),
        )

    def start_w(zz, _):
        for c in wcopies(zz):
            c.start()
        return 0

    lax.fori_loop(0, NZ, start_w, 0)

    c_emb.wait()
    c_gain.wait()
    x[pl.ds(ROWS, XROWS - ROWS), :] = jnp.broadcast_to(emb_s[...], (XROWS - ROWS, D))
    ss[...] = jnp.zeros_like(ss)
    acc[...] = jnp.zeros_like(acc)

    def kstep(k, _):
        for c in xcopies(k):
            c.wait()
        cols = pl.ds(pl.multiple_of(k * KB, KB), KB)
        xf = x[:, cols].astype(F32)
        sq = xf * xf
        total = sq[:, :128]
        for j in range(1, KB // 128):
            total = total + sq[:, j * 128:(j + 1) * 128]
        ss[...] += total
        xg = (xf * gain_s[:, cols]).astype(BF16)
        x[:, cols] = xg
        acc[...] += jnp.dot(xg, wkv_s[cols, :], preferred_element_type=F32)
        return 0

    lax.fori_loop(0, NKB, kstep, 0)
    c_mask.wait()
    c_tab.wait()
    scale = lax.rsqrt(jnp.sum(ss[...], axis=1, keepdims=True) * (1.0 / D) + 1e-05)
    ss[...] = jnp.broadcast_to(scale, (XROWS, 128))
    flags = (mask_s[...] == 1).astype(F32)
    for i in range(ROWS // 128):
        maskc[pl.ds(i * 128, 128), :] = jnp.transpose(
            jnp.broadcast_to(flags[i:i + 1, :], (128, 128)))

    def chosen(ref, lo):
        u = ref[:, lo:lo + HD] * ss[...]
        return jnp.where(maskc[...] > 0.5, u[ROWS:ROWS + 1, :], u[:ROWS, :])

    lane = lax.broadcasted_iota(jnp.int32, (ROWS, HD), 1)

    def rope(u):
        t = tab_s[...]
        r = pltpu.roll(t, HD // 2, 1)
        c = jnp.where(lane < HD // 2, t, r)
        s = jnp.where(lane < HD // 2, -r, t)
        return u * c + pltpu.roll(u, HD // 2, 1) * s

    me = core * NX + xi
    put = jnp.where(diag, me, 8)
    kv[put, 0] = rope(chosen(acc, 0)).astype(BF16)
    kv[put, 1] = chosen(acc, HD).astype(BF16)

    partner = dev(ylo_=oylo, core_=oc)
    swap_k = pltpu.make_async_remote_copy(
        kv.at[8, 0], kv.at[ctx, 0], sw_send.at[0], sw_recv.at[0],
        device_id=partner, device_id_type=MESH)
    swap_v = pltpu.make_async_remote_copy(
        kv.at[8, 1], kv.at[ctx, 1], sw_send.at[1], sw_recv.at[1],
        device_id=partner, device_id_type=MESH)
    swap_q = pltpu.make_async_remote_copy(
        qs.at[1], qs.at[0], sw_send.at[2], sw_recv.at[2],
        device_id=partner, device_id_type=MESH)

    OWN, LEFT, RIGHT, OPP = 0, 1, 2, 3
    offs = (xi, xl, xr, xo)
    myset = jnp.where(diag, 0, 1)
    sends = {}
    n_send = [0]

    def kvcopy(pos_here, pos_there, which, to):
        slot = core * NX + offs[pos_here]
        c = pltpu.make_async_remote_copy(
            kv.at[slot, which], kv.at[slot, which], kv_send.at[n_send[0]],
            kv_recv.at[myset, pos_there, which], device_id=to, device_id_type=MESH)
        n_send[0] += 1
        return c

    to_r, to_l, to_c = dev(x_=xr), dev(x_=xl), dev(core_=oc)
    own_sends = [
        kvcopy(OWN, LEFT, 0, to_r), kvcopy(OWN, RIGHT, 1, to_l),
        kvcopy(OWN, LEFT, 1, to_r), kvcopy(OWN, RIGHT, 0, to_l),
        kvcopy(OWN, OWN, 0, to_c), kvcopy(OWN, OWN, 1, to_c),
    ]
    fwd_k = kvcopy(LEFT, OPP, 0, to_r)
    fwd_v = kvcopy(RIGHT, OPP, 1, to_l)
    core_sends = {(pos, w): kvcopy(pos, pos, w, to_c)
                  for pos in (LEFT, RIGHT, OPP) for w in (0, 1)}

    @pl.when(diag)
    def _():
        for c in own_sends:
            c.start()

    @pl.when(off)
    def _():
        swap_k.start()
        swap_v.start()

    c_wq.wait()
    qacc[...] = jnp.zeros_like(qacc)

    def qstep(k, _):
        cols = pl.ds(pl.multiple_of(k * KB, KB), KB)
        qacc[...] += jnp.dot(x[:, cols], wq_s[cols, :], preferred_element_type=F32)
        return 0

    lax.fori_loop(0, NKB, qstep, 0)
    q_factor = math.log2(math.e) / math.sqrt(HD)
    qs[jnp.where(diag, 0, 1)] = (rope(chosen(qacc, 0)) * q_factor).astype(BF16)

    @pl.when(off)
    def _():
        swap_q.start()
        swap_k.wait_recv()
        swap_v.wait_recv()
        for c in own_sends:
            c.start()
        swap_q.wait_recv()

    def arrived(st, pos, which):
        slot = (ylo if st == 0 else oylo) * NX + offs[pos]
        pltpu.make_async_copy(kv.at[slot, which], kv.at[slot, which],
                              kv_recv.at[st, pos, which]).wait()

    ones = jnp.ones((ROWS, HD), BF16)

    def attend_rows(slot, i, first):
        rows = pl.ds(i * QB, QB)
        s = lax.dot_general(qs[0, rows, :], kv[slot, 0], (((1,), (1,)), ((), ())),
                            preferred_element_type=F32)
        top = jnp.broadcast_to(jnp.max(s, axis=1, keepdims=True), (QB, HD))
        if not first:
            old = m_s[rows, :]
            top = jnp.maximum(top, old)
        m_s[rows, :] = top
        p = jnp.exp2(s - jnp.concatenate([top] * (ROWS // HD), axis=1)).astype(BF16)
        v = jnp.concatenate([kv[slot, 1], ones], axis=1)
        add = jnp.dot(p, v, preferred_element_type=F32)
        if first:
            o_s[rows, :] = add
        else:
            alpha = jnp.exp2(old - top)
            o_s[rows, :] = o_s[rows, :] * jnp.concatenate([alpha, alpha], axis=1) + add

    def attend(st, pos):
        slot = (ylo if st == 0 else oylo) * NX + offs[pos]
        for i in range(ROWS // QB):
            attend_rows(slot, i, st == 0 and pos == OWN)

    for st, mine, other in ((0, diag, off), (1, off, diag)):
        @pl.when(other)
        def _():
            arrived(st, OWN, 0)
            arrived(st, OWN, 1)

        attend(st, OWN)

        for pos, which, fwd in ((LEFT, 0, fwd_k), (RIGHT, 1, fwd_v), (LEFT, 1, None), (RIGHT, 0, None)):
            arrived(st, pos, which)

            @pl.when(mine)
            def _():
                if fwd is not None:
                    fwd.start()
                core_sends[pos, which].start()

        attend(st, LEFT)
        attend(st, RIGHT)
        for which in (0, 1):
            arrived(st, OPP, which)

            @pl.when(mine)
            def _():
                core_sends[OPP, which].start()

        attend(st, OPP)

    hslot = yhi * 2 + ylo
    mcols = pl.ds(pl.multiple_of(hslot * HD, HD), HD)
    dests = [dev(ylo_=core, yhi_=h, core_=c) for h in (yhi, oyhi) for c in (core, oc)]

    def mcopy(r, j):
        rows = pl.ds(r * RB, RB)
        return pltpu.make_async_remote_copy(
            mixed.at[rows], mbuf.at[rows, mcols], m_send.at[j, r], m_recv.at[hslot, r],
            device_id=dests[j], device_id_type=MESH)

    for r in range(R):
        rows = pl.ds(r * RB, RB)
        o = o_s[rows, :]
        mix = (o[:, :HD] / o[:, HD:]).astype(BF16)
        mixed[rows, :] = mix

        @pl.when(off)
        def _():
            mcopy(r, 0).start()

        @pl.when(diag)
        def _():
            mbuf[rows, mcols] = mix

        for j in (1, 2, 3):
            mcopy(r, j).start()

    own_w = wd.at[my_rows]
    pltpu.make_async_copy(own_w, own_w, ld_w.at[0]).wait()
    for n, slot in ((0, yhi * 2 + oc), (1, oyhi * 2), (2, oyhi * 2 + 1)):
        ref = wd.at[pl.ds(pl.multiple_of(slot * HD, HD), HD)]
        pltpu.make_async_copy(ref, ref, w_recv.at[n]).wait()

    def hops(d, r):
        return NZ // 2 if (d == 0) == (r < R // 2) else NZ // 2 - 1

    def zcopy(d, r, i):
        return pltpu.make_async_remote_copy(
            sb.at[d, r, i], rb.at[d, r, i], z_send.at[d, r, i], z_recv.at[d, r, i],
            device_id=dev(z_=zr if d == 0 else zl), device_id_type=MESH)

    def piece(r, dest):
        return part[pl.ds(r * RB, RB), pl.ds(pl.multiple_of(dest * HD, HD), HD)]

    def partial(r):
        rows = pl.ds(r * RB, RB)
        for h in range(4):
            def wait_slot():
                ref = mbuf.at[rows, pl.ds(h * HD, HD)]
                pltpu.make_async_copy(ref, ref, m_recv.at[h, r]).wait()

            pl.when(jnp.logical_or(off, hslot != h))(wait_slot)
        part[rows, :] = jnp.dot(mbuf[rows, :], wd[...], preferred_element_type=F32)

    steps = NZ // 2
    for w in range(R + steps):
        if w < R:
            partial(w)
        for r in range(R):
            i = w - r
            if i < 0 or i > steps:
                continue
            for d in (0, 1):
                n = hops(d, r)
                if i >= n:
                    continue
                sign = 1 if d == 0 else -1
                dest = lax.rem(z + NZ + sign * (n - i), NZ)
                val = piece(r, dest)
                if i > 0:
                    zcopy(d, r, i - 1).wait_recv()
                    val = val + rb[d, r, i - 1].astype(F32)
                sb[d, r, i] = val.astype(BF16)
                zcopy(d, r, i).start()
            if i == steps:
                val = piece(r, z)
                for d in (0, 1):
                    last = hops(d, r) - 1
                    zcopy(d, r, last).wait_recv()
                    val = val + rb[d, r, last].astype(F32)
                out[pl.ds(r * RB, RB), :] = val.astype(BF16)

    for n, c in ((0, oc), (1, 0), (2, 1)):
        pltpu.make_async_copy(own_w, own_w, w_send.at[n]).wait()

    @pl.when(off)
    def _():
        for c in (swap_k, swap_v, swap_q):
            c.wait_send()

    for c in own_sends + [fwd_k, fwd_v] + list(core_sends.values()):
        c.wait_send()
    for r in range(R):
        @pl.when(off)
        def _():
            mcopy(r, 0).wait_send()

        for j in (1, 2, 3):
            mcopy(r, j).wait_send()
        for d in (0, 1):
            for i in range(hops(d, r)):
                zcopy(d, r, i).wait_send()


def on_device(hidden, mask_flags, mask_embed, norm_gain, w_query, w_key, w_value, w_out):
    any_spec = pl.BlockSpec(memory_space=pl.ANY)
    dma = pltpu.SemaphoreType.DMA
    return pl.pallas_call(
        kernel,
        out_shape=jax.ShapeDtypeStruct((ROWS, HD), BF16),
        in_specs=[any_spec] * 9,
        out_specs=pl.BlockSpec(memory_space=pltpu.VMEM),
        scratch_shapes=[
            pltpu.VMEM((XROWS, D), BF16),
            pltpu.VMEM((D, 2 * HD), BF16),
            pltpu.VMEM((D, HD), BF16),
            pltpu.VMEM((1, D), BF16),
            pltpu.VMEM((1, D), F32),
            pltpu.VMEM((ROWS // 128, 128), jnp.int32),
            pltpu.VMEM((ROWS, HD), F32),
            pltpu.VMEM((ROWS, 128), F32),
            pltpu.VMEM((XROWS, 128), F32),
            pltpu.VMEM((XROWS, 2 * HD), F32),
            pltpu.VMEM((XROWS, HD), F32),
            pltpu.VMEM((9, 2, ROWS, HD), BF16),
            pltpu.VMEM((2, ROWS, HD), BF16),
            pltpu.VMEM((ROWS, HD), F32),
            pltpu.VMEM((ROWS, 2 * HD), F32),
            pltpu.VMEM((ROWS, HD), BF16),
            pltpu.VMEM((ROWS, 4 * HD), BF16),
            pltpu.VMEM((4 * HD, NZ * HD), BF16),
            pltpu.VMEM((ROWS, NZ * HD), F32),
            pltpu.VMEM((2, R, NZ // 2, RB, HD), BF16),
            pltpu.VMEM((2, R, NZ // 2, RB, HD), BF16),
            dma((NKB,)), dma((NKB,)), dma((NKB,)), dma((5,)), dma((1,)),
            dma((3,)), dma((3,)), dma((3,)), dma((3,)),
            dma((14,)), dma((2, 4, 2)), dma((4, R)), dma((4, R)),
            dma((2, R, NZ // 2)), dma((2, R, NZ // 2)),
        ],
        compiler_params=pltpu.CompilerParams(
            collective_id=0, has_side_effects=True, vmem_limit_bytes=48 * 1024 * 1024),
    )(hidden, mask_flags.reshape(ROWS // 128, 128), mask_embed.reshape(1, D),
      norm_gain.reshape(1, D), w_query, w_key, w_value, w_out, jnp.asarray(rope_table()))


def solution(mesh):
    in_specs = (
        P("ctx", None),
        P("ctx"),
        P(),
        P(),
        P(None, "tp"),
        P(None, "tp"),
        P(None, "tp"),
        P("tp", None),
    )
    return jax.shard_map(
        on_device, mesh=mesh, in_specs=in_specs, out_specs=P("ctx", "tp"), check_vma=False
    )
```

time: 259 us -> 69.3 us (0.27)
  the two profiles are of different devices: /device:TPU:6 before, /device:TPU:64 now
where the time goes in v1:
time: 69.3 us; the launch traced here: 69 us
  Pallas kernels  61.3 us (88%)
  local copies, waits for them, and re-layouts  7.66 us (11%)
    pallas_call x1, Pallas kernels, on_device(): pl.pallas_call(kernel, out_shape=jax.ShapeDtypeStruct((ROWS, HD), BF16),...  61.3 us
    unnamed x13, local copies, waits for them, and re-layouts  6.95 us

profile of v1, /device:TPU:64, one launch (start us, length us, event | category | flops | bytes accessed | tf_op | source)
XLA Modules:
  0.0 69.0 jit_solution(5264083129336818155)
XLA Ops:
  0.0 0.7 %reshape.10.emb = bf16[1,4096]{1,0:T(2,128)(2,1)S(1)} reshape(bf16[4096]{0:T(1024)(128)(2,1)} %param.11) | data formatting | bytes 16384 | tf_op jit(solution)/shard_map/reshape | solution.py:435
  0.7 0.0 copy-start
  0.7 1.2 %copy-done = bf16[4096,128]{1,0:T(8,128)(2,1)S(1)} copy-done((bf16[4096,128]{1,0:T(8,128)(2,1)S(1)}, bf16[4096,128]{1,0:T(8,128)(2,1)}, u32[]{:S(2)}) %copy-start) | copy-done | bytes 1048600
  1.9 0.0 copy-start.1
  1.9 1.2 %copy-done.1 = bf16[4096,128]{1,0:T(8,128)(2,1)S(1)} copy-done((bf16[4096,128]{1,0:T(8,128)(2,1)S(1)}, bf16[4096,128]{1,0:T(8,128)(2,1)}, u32[]{:S(2)}) %copy-start.1) | copy-done | bytes 1048600
  3.2 0.0 copy-start.2
  3.2 1.2 %copy-done.2 = bf16[4096,128]{1,0:T(8,128)(2,1)S(1)} copy-done((bf16[4096,128]{1,0:T(8,128)(2,1)S(1)}, bf16[4096,128]{1,0:T(8,128)(2,1)}, u32[]{:S(2)}) %copy-start.2) | copy-done | bytes 1048600
  4.4 0.0 copy-start.3
  4.4 1.2 %copy-done.3 = bf16[128,4096]{1,0:T(8,128)(2,1)S(1)} copy-done((bf16[128,4096]{1,0:T(8,128)(2,1)S(1)}, bf16[128,4096]{1,0:T(8,128)(2,1)}, u32[]{:S(2)}) %copy-start.3) | copy-done | bytes 1048600
  5.6 0.0 copy-start.4
  5.6 0.7 %copy-done.4 = f32[4096]{0:T(1024)S(1)} copy-done((f32[4096]{0:T(1024)S(1)}, f32[4096]{0:T(1024)}, u32[]{:S(2)}) %copy-start.4) | copy-done | bytes 16408
  6.3 0.0 copy-start.5
  6.3 0.7 copy-done.5
  7.0 61.3 %shard_map.91 = bf16[512,128]{1,0:T(8,128)(2,1)S(1)} custom-call(bf16[512,4096]{1,0:T(8,128)(2,1)} %hid.1, s32[4,128]{1,0:T(4,128)S(1)} %bitcast.3, bf16[1,4096]{1,0:T(2,128)(2,1)S(1)} %reshape.10.emb, f32[1,4096]{1,0:T(1,128)S(1)} %bitcast.2, bf16[4096,128]{1,0:T(8,128)(2,1)S(1)} %copy-done, bf16[4096,128]{1,0:T(8,128)(2,1)S(1)} %copy-done.1, ...), custom_call_target="tpu_custom_call" | custom-call | tf_op jit(solution)/shard_map/pallas_call | solution.py:401
  68.3 0.7 copy.11
Async XLA Ops:
  0.7 1.2 %copy-start = (bf16[4096,128]{1,0:T(8,128)(2,1)S(1)}, bf16[4096,128]{1,0:T(8,128)(2,1)}, u32[]{:S(2)}) copy-start(bf16[4096,128]{1,0:T(8,128)(2,1)} %wq.1) | copy-start | bytes 3145732
  1.9 1.2 %copy-start.1 = (bf16[4096,128]{1,0:T(8,128)(2,1)S(1)}, bf16[4096,128]{1,0:T(8,128)(2,1)}, u32[]{:S(2)}) copy-start(bf16[4096,128]{1,0:T(8,128)(2,1)} %wk.1) | copy-start | bytes 3145732
  3.2 1.2 %copy-start.2 = (bf16[4096,128]{1,0:T(8,128)(2,1)S(1)}, bf16[4096,128]{1,0:T(8,128)(2,1)}, u32[]{:S(2)}) copy-start(bf16[4096,128]{1,0:T(8,128)(2,1)} %wv.1) | copy-start | bytes 3145732
  4.4 1.2 %copy-start.3 = (bf16[128,4096]{1,0:T(8,128)(2,1)S(1)}, bf16[128,4096]{1,0:T(8,128)(2,1)}, u32[]{:S(2)}) copy-start(bf16[128,4096]{1,0:T(8,128)(2,1)} %wo.1) | copy-start | bytes 3145732
  5.6 0.7 %copy-start.4 = (f32[4096]{0:T(1024)S(1)}, f32[4096]{0:T(1024)}, u32[]{:S(2)}) copy-start(f32[4096]{0:T(1024)} %param.12) | copy-start | bytes 49156
  6.3 0.7 copy-start.5

commit v2 on v1

--- a/solution.py
+++ b/solution.py
@@ -35,7 +35,7 @@
            x, wkv_s, wq_s, emb_s, gain_s, mask_s, tab_s, maskc, ss, acc, qacc,
            kv, qs, m_s, o_s, mixed, mbuf, wd, part, rb, sb,
            ld_x, ld_k, ld_v, ld_s, ld_w, w_send, w_recv, sw_send, sw_recv,
-           kv_send, kv_recv, m_send, m_recv, z_send, z_recv):
+           kv_send, kv_recv, m_send, m_recv, p_send, z_send, z_recv):
     ctx = lax.axis_index("ctx")
     tp = lax.axis_index("tp")
     xi, ylo = lax.rem(ctx, NX), lax.div(ctx, NX)
@@ -51,7 +51,6 @@
     zr, zl = lax.rem(z + 1, NZ), lax.rem(z + NZ - 1, NZ)
     oc, oylo, oyhi = 1 - core, 1 - ylo, 1 - yhi
 
-    loads = []
     c_gain = pltpu.make_async_copy(gain, gain_s, ld_s.at[0])
     c_emb = pltpu.make_async_copy(emb, emb_s, ld_s.at[1])
     c_mask = pltpu.make_async_copy(mask, mask_s, ld_s.at[2])
@@ -80,13 +79,12 @@
     c_wq.start()
 
     barrier = pltpu.get_barrier_semaphore()
-    partners = [dev(x_=xr), dev(x_=xl), dev(z_=zr), dev(z_=zl), dev(core_=oc)]
+    partners = [dev(x_=xr), dev(x_=xl), dev(x_=xo), dev(z_=zr), dev(z_=zl), dev(core_=oc)]
     for c in (0, 1):
         partners += [dev(ylo_=oylo, core_=c), dev(yhi_=oyhi, core_=c),
                      dev(ylo_=oylo, yhi_=oyhi, core_=c)]
     for p in partners:
         pl.semaphore_signal(barrier, inc=1, device_id=p, device_id_type=MESH)
-    pl.semaphore_wait(barrier, len(partners))
 
     my_rows = pl.ds(pl.multiple_of((yhi * 2 + core) * HD, HD), HD)
 
@@ -115,11 +113,9 @@
             c.start()
         return 0
 
-    lax.fori_loop(0, NZ, start_w, 0)
-
     c_emb.wait()
     c_gain.wait()
-    x[pl.ds(ROWS, XROWS - ROWS), :] = jnp.broadcast_to(emb_s[...], (XROWS - ROWS, D))
+    x[pl.ds(ROWS, XROWS - ROWS), :] = jnp.broadcast_to(emb_s[...].reshape(1, D), (XROWS - ROWS, D))
     ss[...] = jnp.zeros_like(ss)
     acc[...] = jnp.zeros_like(acc)
 
@@ -166,6 +162,8 @@
     kv[put, 0] = rope(chosen(acc, 0)).astype(BF16)
     kv[put, 1] = chosen(acc, HD).astype(BF16)
 
+    pl.semaphore_wait(barrier, len(partners))
+
     partner = dev(ylo_=oylo, core_=oc)
     swap_k = pltpu.make_async_remote_copy(
         kv.at[8, 0], kv.at[ctx, 0], sw_send.at[0], sw_recv.at[0],
@@ -180,15 +178,14 @@
     OWN, LEFT, RIGHT, OPP = 0, 1, 2, 3
     offs = (xi, xl, xr, xo)
     myset = jnp.where(diag, 0, 1)
-    sends = {}
     n_send = [0]
 
-    def kvcopy(pos_here, pos_there, which, to):
+    def kvcopy(pos_here, pos_there, which, to, n=None):
         slot = core * NX + offs[pos_here]
         c = pltpu.make_async_remote_copy(
-            kv.at[slot, which], kv.at[slot, which], kv_send.at[n_send[0]],
+            kv.at[slot, which], kv.at[slot, which], kv_send.at[n_send[0] if n is None else n],
             kv_recv.at[myset, pos_there, which], device_id=to, device_id_type=MESH)
-        n_send[0] += 1
+        n_send[0] += n is None
         return c
 
     to_r, to_l, to_c = dev(x_=xr), dev(x_=xl), dev(core_=oc)
@@ -199,6 +196,8 @@
     ]
     fwd_k = kvcopy(LEFT, OPP, 0, to_r)
     fwd_v = kvcopy(RIGHT, OPP, 1, to_l)
+    to_o = dev(x_=xo)
+    far_sends = [kvcopy(OWN, OPP, w, to_o, n_send[0] - 2 + w) for w in (0, 1)]
     core_sends = {(pos, w): kvcopy(pos, pos, w, to_c)
                   for pos in (LEFT, RIGHT, OPP) for w in (0, 1)}
 
@@ -211,6 +210,8 @@
     def _():
         swap_k.start()
         swap_v.start()
+
+    lax.fori_loop(0, NZ, start_w, 0)
 
     c_wq.wait()
     qacc[...] = jnp.zeros_like(qacc)
@@ -229,7 +230,7 @@
         swap_q.start()
         swap_k.wait_recv()
         swap_v.wait_recv()
-        for c in own_sends:
+        for c in far_sends + own_sends:
             c.start()
         swap_q.wait_recv()
 
@@ -276,7 +277,7 @@
 
             @pl.when(mine)
             def _():
-                if fwd is not None:
+                if fwd is not None and st == 0:
                     fwd.start()
                 core_sends[pos, which].start()
 
@@ -289,34 +290,38 @@
             def _():
                 core_sends[OPP, which].start()
 
-        attend(st, OPP)
+        if st == 0:
+            attend(st, OPP)
 
     hslot = yhi * 2 + ylo
     mcols = pl.ds(pl.multiple_of(hslot * HD, HD), HD)
-    dests = [dev(ylo_=core, yhi_=h, core_=c) for h in (yhi, oyhi) for c in (core, oc)]
 
     def mcopy(r, j):
         rows = pl.ds(r * RB, RB)
+        to = (dev(ylo_=core, yhi_=yhi, core_=r % 2), dev(ylo_=core, yhi_=oyhi, core_=r % 2), to_c)[j]
         return pltpu.make_async_remote_copy(
-            mixed.at[rows], mbuf.at[rows, mcols], m_send.at[j, r], m_recv.at[hslot, r],
-            device_id=dests[j], device_id_type=MESH)
-
-    for r in range(R):
-        rows = pl.ds(r * RB, RB)
-        o = o_s[rows, :]
-        mix = (o[:, :HD] / o[:, HD:]).astype(BF16)
-        mixed[rows, :] = mix
-
-        @pl.when(off)
-        def _():
-            mcopy(r, 0).start()
-
-        @pl.when(diag)
-        def _():
-            mbuf[rows, mcols] = mix
-
-        for j in (1, 2, 3):
-            mcopy(r, j).start()
+            mixed.at[rows], mbuf.at[rows, mcols], m_send.at[j % 2, r], m_recv.at[hslot, r],
+            device_id=to, device_id_type=MESH)
+
+    last = oylo * NX + xo
+    for i in range(ROWS // QB):
+        attend_rows(last, i, False)
+        for r in range(i * R * QB // ROWS, (i + 1) * R * QB // ROWS):
+            rows = pl.ds(r * RB, RB)
+            o = o_s[rows, :]
+            mix = (o[:, :HD] / o[:, HD:]).astype(BF16)
+            mixed[rows, :] = mix
+
+            @pl.when(off)
+            def _():
+                mcopy(r, 0).start()
+
+            @pl.when(diag)
+            def _():
+                mbuf[rows, mcols] = mix
+                mcopy(r, 2).start()
+
+            mcopy(r, 1).start()
 
     own_w = wd.at[my_rows]
     pltpu.make_async_copy(own_w, own_w, ld_w.at[0]).wait()
@@ -334,6 +339,11 @@
 
     def piece(r, dest):
         return part[pl.ds(r * RB, RB), pl.ds(pl.multiple_of(dest * HD, HD), HD)]
+
+    def mpass(h, r):
+        ref = mbuf.at[pl.ds(r * RB, RB), pl.ds(h * HD, HD)]
+        return pltpu.make_async_remote_copy(
+            ref, ref, p_send.at[h, r], m_recv.at[h, r], device_id=to_c, device_id_type=MESH)
 
     def partial(r):
         rows = pl.ds(r * RB, RB)
@@ -342,37 +352,42 @@
                 ref = mbuf.at[rows, pl.ds(h * HD, HD)]
                 pltpu.make_async_copy(ref, ref, m_recv.at[h, r]).wait()
 
+            def pass_on():
+                mpass(h, r).start()
+
             pl.when(jnp.logical_or(off, hslot != h))(wait_slot)
+            pl.when(jnp.logical_and(core == r % 2, hslot != h))(pass_on)
         part[rows, :] = jnp.dot(mbuf[rows, :], wd[...], preferred_element_type=F32)
 
     steps = NZ // 2
-    for w in range(R + steps):
-        if w < R:
-            partial(w)
+
+    def zstep(r, i):
+        for d in (0, 1):
+            n = hops(d, r)
+            if i >= n:
+                continue
+            sign = 1 if d == 0 else -1
+            dest = lax.rem(z + NZ + sign * (n - i), NZ)
+            val = piece(r, dest)
+            if i > 0:
+                zcopy(d, r, i - 1).wait_recv()
+                val = val + rb[d, r, i - 1].astype(F32)
+            sb[d, r, i] = val.astype(BF16)
+            zcopy(d, r, i).start()
+        if i == steps:
+            val = piece(r, z)
+            for d in (0, 1):
+                end = hops(d, r) - 1
+                zcopy(d, r, end).wait_recv()
+                val = val + rb[d, r, end].astype(F32)
+            out[pl.ds(r * RB, RB), :] = val.astype(BF16)
+
+    for r in range(R):
+        partial(r)
+        zstep(r, 0)
+    for i in range(1, steps + 1):
         for r in range(R):
-            i = w - r
-            if i < 0 or i > steps:
-                continue
-            for d in (0, 1):
-                n = hops(d, r)
-                if i >= n:
-                    continue
-                sign = 1 if d == 0 else -1
-                dest = lax.rem(z + NZ + sign * (n - i), NZ)
-                val = piece(r, dest)
-                if i > 0:
-                    zcopy(d, r, i - 1).wait_recv()
-                    val = val + rb[d, r, i - 1].astype(F32)
-                sb[d, r, i] = val.astype(BF16)
-                zcopy(d, r, i).start()
-            if i == steps:
-                val = piece(r, z)
-                for d in (0, 1):
-                    last = hops(d, r) - 1
-                    zcopy(d, r, last).wait_recv()
-                    val = val + rb[d, r, last].astype(F32)
-                out[pl.ds(r * RB, RB), :] = val.astype(BF16)
-
+            zstep(r, i)
     for n, c in ((0, oc), (1, 0), (2, 1)):
         pltpu.make_async_copy(own_w, own_w, w_send.at[n]).wait()
 
@@ -384,12 +399,10 @@
     for c in own_sends + [fwd_k, fwd_v] + list(core_sends.values()):
         c.wait_send()
     for r in range(R):
-        @pl.when(off)
-        def _():
-            mcopy(r, 0).wait_send()
-
-        for j in (1, 2, 3):
-            mcopy(r, j).wait_send()
+        mcopy(r, 0).wait_send()
+        mcopy(r, 1).wait_send()
+        for h in range(4):
+            pl.when(jnp.logical_and(core == r % 2, hslot != h))(mpass(h, r).wait_send)
         for d in (0, 1):
             for i in range(hops(d, r)):
                 zcopy(d, r, i).wait_send()
@@ -407,7 +420,7 @@
             pltpu.VMEM((XROWS, D), BF16),
             pltpu.VMEM((D, 2 * HD), BF16),
             pltpu.VMEM((D, HD), BF16),
-            pltpu.VMEM((1, D), BF16),
+            pltpu.VMEM((D,), BF16),
             pltpu.VMEM((1, D), F32),
             pltpu.VMEM((ROWS // 128, 128), jnp.int32),
             pltpu.VMEM((ROWS, HD), F32),
@@ -427,12 +440,12 @@
             pltpu.VMEM((2, R, NZ // 2, RB, HD), BF16),
             dma((NKB,)), dma((NKB,)), dma((NKB,)), dma((5,)), dma((1,)),
             dma((3,)), dma((3,)), dma((3,)), dma((3,)),
-            dma((14,)), dma((2, 4, 2)), dma((4, R)), dma((4, R)),
+            dma((14,)), dma((2, 4, 2)), dma((2, R)), dma((4, R)), dma((4, R)),
             dma((2, R, NZ // 2)), dma((2, R, NZ // 2)),
         ],
         compiler_params=pltpu.CompilerParams(
-            collective_id=0, has_side_effects=True, vmem_limit_bytes=48 * 1024 * 1024),
-    )(hidden, mask_flags.reshape(ROWS // 128, 128), mask_embed.reshape(1, D),
+            collective_id=0, has_side_effects=True, vmem_limit_bytes=62 * 1024 * 1024),
+    )(hidden, mask_flags.reshape(ROWS // 128, 128), mask_embed,
       norm_gain.reshape(1, D), w_query, w_key, w_value, w_out, jnp.asarray(rope_table()))
 
 

time: 69.3 us -> 55.3 us (0.80)
  the two profiles are of different devices: /device:TPU:64 before, /device:TPU:6 now
where the time goes in v2:
time: 55.3 us; the launch traced here: 55.2 us
  Pallas kernels  53.6 us (97%)
  local copies, waits for them, and re-layouts  1.57 us (3%)
    pallas_call x1, Pallas kernels, on_device(): pl.pallas_call(kernel, out_shape=jax.ShapeDtypeStruct((ROWS, HD), BF16),...  53.6 us
    unnamed x1, local copies, waits for them, and re-layouts  1.57 us

profile of v2, /device:TPU:6, one launch (start us, length us, event | category | flops | bytes accessed | tf_op | source)
XLA Modules:
  0.0 55.2 jit_solution(2805485308079693228)
XLA Ops:
  0.0 53.6 %shard_map.91 = bf16[512,128]{1,0:T(8,128)(2,1)} custom-call(bf16[512,4096]{1,0:T(8,128)(2,1)} %hid.1, s32[4,128]{1,0:T(4,128)} %bitcast.3, bf16[4096]{0:T(1024)(128)(2,1)} %emb.1, f32[1,4096]{1,0:T(1,128)} %bitcast.2, bf16[4096,128]{1,0:T(8,128)(2,1)} %wq.1, bf16[4096,128]{1,0:T(8,128)(2,1)} %wk.1, bf16[4096,128]{1,0:T(8,128)(2,1)} %wv.1, ...), custom_call_target="tpu_custom_call" | custom-call | tf_op jit(solution)/shard_map/pallas_call | solution.py:414
  53.6 1.6 %copy.11 = bf16[512,128]{1,0:T(8,128)(2,1)} copy(bf16[512,128]{1,0:T(8,128)(2,1)} %shard_map.91) | data formatting | bytes 262144

commit v3 on v2

--- a/solution.py
+++ b/solution.py
@@ -13,8 +13,9 @@
 SEQ = 4096
 ROWS = 512
 XROWS = 528
-KB = 512
+KB = 1024
 NKB = D // KB
+KQ = 512
 R = 4
 RB = ROWS // R
 QB = 256
@@ -35,7 +36,7 @@
            x, wkv_s, wq_s, emb_s, gain_s, mask_s, tab_s, maskc, ss, acc, qacc,
            kv, qs, m_s, o_s, mixed, mbuf, wd, part, rb, sb,
            ld_x, ld_k, ld_v, ld_s, ld_w, w_send, w_recv, sw_send, sw_recv,
-           kv_send, kv_recv, m_send, m_recv, p_send, z_send, z_recv):
+           kv_send, kv_recv, opp_recv, m_send, m_recv, p_send, z_send, z_recv):
     ctx = lax.axis_index("ctx")
     tp = lax.axis_index("tp")
     xi, ylo = lax.rem(ctx, NX), lax.div(ctx, NX)
@@ -49,6 +50,7 @@
     xr, xl = lax.rem(xi + 1, NX), lax.rem(xi + NX - 1, NX)
     xo = lax.rem(xi + 2, NX)
     zr, zl = lax.rem(z + 1, NZ), lax.rem(z + NZ - 1, NZ)
+    zr2, zl2 = lax.rem(z + 2, NZ), lax.rem(z + NZ - 2, NZ)
     oc, oylo, oyhi = 1 - core, 1 - ylo, 1 - yhi
 
     c_gain = pltpu.make_async_copy(gain, gain_s, ld_s.at[0])
@@ -79,7 +81,7 @@
     c_wq.start()
 
     barrier = pltpu.get_barrier_semaphore()
-    partners = [dev(x_=xr), dev(x_=xl), dev(x_=xo), dev(z_=zr), dev(z_=zl), dev(core_=oc)]
+    partners = [dev(x_=xr), dev(x_=xl), dev(z_=zr2), dev(z_=zl2), dev(z_=zr), dev(z_=zl), dev(core_=oc)]
     for c in (0, 1):
         partners += [dev(ylo_=oylo, core_=c), dev(yhi_=oyhi, core_=c),
                      dev(ylo_=oylo, yhi_=oyhi, core_=c)]
@@ -178,32 +180,50 @@
     OWN, LEFT, RIGHT, OPP = 0, 1, 2, 3
     offs = (xi, xl, xr, xo)
     myset = jnp.where(diag, 0, 1)
-    n_send = [0]
-
-    def kvcopy(pos_here, pos_there, which, to, n=None):
-        slot = core * NX + offs[pos_here]
-        c = pltpu.make_async_remote_copy(
-            kv.at[slot, which], kv.at[slot, which], kv_send.at[n_send[0] if n is None else n],
-            kv_recv.at[myset, pos_there, which], device_id=to, device_id_type=MESH)
-        n_send[0] += n is None
-        return c
-
     to_r, to_l, to_c = dev(x_=xr), dev(x_=xl), dev(core_=oc)
+    HALF = ROWS // 2
+
+    def block(slot, which, half):
+        if half is None:
+            return kv.at[slot, which]
+        return kv.at[slot, which, pl.ds(half * HALF, HALF)]
+
+    def kvcopy(pos, which, half, n, recv, to):
+        ref = block(core * NX + offs[pos], which, half)
+        return pltpu.make_async_remote_copy(
+            ref, ref, kv_send.at[n], recv, device_id=to, device_id_type=MESH)
+
     own_sends = [
-        kvcopy(OWN, LEFT, 0, to_r), kvcopy(OWN, RIGHT, 1, to_l),
-        kvcopy(OWN, LEFT, 1, to_r), kvcopy(OWN, RIGHT, 0, to_l),
-        kvcopy(OWN, OWN, 0, to_c), kvcopy(OWN, OWN, 1, to_c),
-    ]
-    fwd_k = kvcopy(LEFT, OPP, 0, to_r)
-    fwd_v = kvcopy(RIGHT, OPP, 1, to_l)
-    to_o = dev(x_=xo)
-    far_sends = [kvcopy(OWN, OPP, w, to_o, n_send[0] - 2 + w) for w in (0, 1)]
-    core_sends = {(pos, w): kvcopy(pos, pos, w, to_c)
-                  for pos in (LEFT, RIGHT, OPP) for w in (0, 1)}
+        (kvcopy(OWN, w, None, 3 * w, kv_recv.at[myset, LEFT, w], to_r),
+         kvcopy(OWN, w, None, 3 * w + 1, kv_recv.at[myset, RIGHT, w], to_l),
+         kvcopy(OWN, w, None, 3 * w + 2, kv_recv.at[myset, OWN, w], to_c)) for w in (0, 1)]
+    passes = {}
+    for w in (0, 1):
+        passes[LEFT, w] = (
+            kvcopy(LEFT, w, 0, 6 + w, opp_recv.at[myset, w, 0], to_r),
+            kvcopy(LEFT, w, None, 8 + w, kv_recv.at[myset, LEFT, w], to_c))
+        passes[RIGHT, w] = (
+            kvcopy(RIGHT, w, 1, 10 + w, opp_recv.at[myset, w, 1], to_l),
+            kvcopy(RIGHT, w, None, 12 + w, kv_recv.at[myset, RIGHT, w], to_c))
+        for h in (0, 1):
+            passes[OPP, w, h] = (
+                kvcopy(OPP, w, h, 14 + 2 * w + h, opp_recv.at[myset, w, h], to_c),)
+
+    def slot_of(st, pos):
+        return (ylo if st == 0 else oylo) * NX + offs[pos]
+
+    def arrived(st, pos, w, h=None):
+        ref = block(slot_of(st, pos), w, h)
+        sem = kv_recv.at[st, pos, w] if h is None else opp_recv.at[st, w, h]
+        pltpu.make_async_copy(ref, ref, sem).wait()
+
+    def pass_on(*key):
+        for c in passes[key]:
+            c.start()
 
     @pl.when(diag)
     def _():
-        for c in own_sends:
+        for c in own_sends[0] + own_sends[1]:
             c.start()
 
     @pl.when(off)
@@ -217,27 +237,24 @@
     qacc[...] = jnp.zeros_like(qacc)
 
     def qstep(k, _):
-        cols = pl.ds(pl.multiple_of(k * KB, KB), KB)
+        cols = pl.ds(pl.multiple_of(k * KQ, KQ), KQ)
         qacc[...] += jnp.dot(x[:, cols], wq_s[cols, :], preferred_element_type=F32)
         return 0
 
-    lax.fori_loop(0, NKB, qstep, 0)
+    lax.fori_loop(0, D // KQ, qstep, 0)
     q_factor = math.log2(math.e) / math.sqrt(HD)
     qs[jnp.where(diag, 0, 1)] = (rope(chosen(qacc, 0)) * q_factor).astype(BF16)
 
     @pl.when(off)
     def _():
         swap_q.start()
-        swap_k.wait_recv()
-        swap_v.wait_recv()
-        for c in far_sends + own_sends:
-            c.start()
+        for swap, copies in ((swap_k, own_sends[0]), (swap_v, own_sends[1])):
+            swap.wait_recv()
+            for c in copies:
+                c.start()
         swap_q.wait_recv()
-
-    def arrived(st, pos, which):
-        slot = (ylo if st == 0 else oylo) * NX + offs[pos]
-        pltpu.make_async_copy(kv.at[slot, which], kv.at[slot, which],
-                              kv_recv.at[st, pos, which]).wait()
+        for w in (0, 1):
+            arrived(0, OWN, w)
 
     ones = jnp.ones((ROWS, HD), BF16)
 
@@ -260,38 +277,73 @@
             o_s[rows, :] = o_s[rows, :] * jnp.concatenate([alpha, alpha], axis=1) + add
 
     def attend(st, pos):
-        slot = (ylo if st == 0 else oylo) * NX + offs[pos]
         for i in range(ROWS // QB):
-            attend_rows(slot, i, st == 0 and pos == OWN)
-
-    for st, mine, other in ((0, diag, off), (1, off, diag)):
-        @pl.when(other)
-        def _():
-            arrived(st, OWN, 0)
-            arrived(st, OWN, 1)
-
-        attend(st, OWN)
-
-        for pos, which, fwd in ((LEFT, 0, fwd_k), (RIGHT, 1, fwd_v), (LEFT, 1, None), (RIGHT, 0, None)):
-            arrived(st, pos, which)
-
-            @pl.when(mine)
-            def _():
-                if fwd is not None and st == 0:
-                    fwd.start()
-                core_sends[pos, which].start()
-
-        attend(st, LEFT)
-        attend(st, RIGHT)
-        for which in (0, 1):
-            arrived(st, OPP, which)
-
-            @pl.when(mine)
-            def _():
-                core_sends[OPP, which].start()
-
-        if st == 0:
-            attend(st, OPP)
+            attend_rows(slot_of(st, pos), i, st == 0 and pos == OWN)
+
+    def opposite(st, mine):
+        for w in (0, 1):
+            for h in (0, 1):
+                arrived(st, OPP, w, h)
+                if mine:
+                    pass_on(OPP, w, h)
+
+    attend(0, OWN)
+
+    @pl.when(diag)
+    def _():
+        for w in (0, 1):
+            for pos in (LEFT, RIGHT):
+                arrived(0, pos, w)
+                pass_on(pos, w)
+
+    @pl.when(off)
+    def _():
+        for pos in (LEFT, RIGHT):
+            arrived(1, pos, 0)
+            pass_on(pos, 0)
+        for w in (0, 1):
+            for pos in (LEFT, RIGHT):
+                arrived(0, pos, w)
+
+    attend(0, LEFT)
+    attend(0, RIGHT)
+
+    @pl.when(diag)
+    def _():
+        opposite(0, True)
+
+    @pl.when(off)
+    def _():
+        for pos in (LEFT, RIGHT):
+            arrived(1, pos, 1)
+            pass_on(pos, 1)
+        opposite(0, False)
+
+    attend(0, OPP)
+
+    @pl.when(diag)
+    def _():
+        for w in (0, 1):
+            arrived(1, OWN, w)
+
+    attend(1, OWN)
+
+    @pl.when(diag)
+    def _():
+        for w in (0, 1):
+            for pos in (LEFT, RIGHT):
+                arrived(1, pos, w)
+
+    attend(1, LEFT)
+    attend(1, RIGHT)
+
+    @pl.when(off)
+    def _():
+        opposite(1, True)
+
+    @pl.when(diag)
+    def _():
+        opposite(1, False)
 
     hslot = yhi * 2 + ylo
     mcols = pl.ds(pl.multiple_of(hslot * HD, HD), HD)
@@ -303,9 +355,8 @@
             mixed.at[rows], mbuf.at[rows, mcols], m_send.at[j % 2, r], m_recv.at[hslot, r],
             device_id=to, device_id_type=MESH)
 
-    last = oylo * NX + xo
     for i in range(ROWS // QB):
-        attend_rows(last, i, False)
+        attend_rows(slot_of(1, OPP), i, False)
         for r in range(i * R * QB // ROWS, (i + 1) * R * QB // ROWS):
             rows = pl.ds(r * RB, RB)
             o = o_s[rows, :]
@@ -329,13 +380,14 @@
         ref = wd.at[pl.ds(pl.multiple_of(slot * HD, HD), HD)]
         pltpu.make_async_copy(ref, ref, w_recv.at[n]).wait()
 
-    def hops(d, r):
+    def reaches(d, r):
         return NZ // 2 if (d == 0) == (r < R // 2) else NZ // 2 - 1
 
-    def zcopy(d, r, i):
+    def zcopy(d, r, t):
+        to = (zr2, zl2)[d] if t == 4 else (zr, zl)[d]
         return pltpu.make_async_remote_copy(
-            sb.at[d, r, i], rb.at[d, r, i], z_send.at[d, r, i], z_recv.at[d, r, i],
-            device_id=dev(z_=zr if d == 0 else zl), device_id_type=MESH)
+            sb.at[d, r, t - 1], rb.at[d, r, t - 1], z_send.at[d, r, t - 1], z_recv.at[d, r, t - 1],
+            device_id=dev(z_=to), device_id_type=MESH)
 
     def piece(r, dest):
         return part[pl.ds(r * RB, RB), pl.ds(pl.multiple_of(dest * HD, HD), HD)]
@@ -359,35 +411,32 @@
             pl.when(jnp.logical_and(core == r % 2, hslot != h))(pass_on)
         part[rows, :] = jnp.dot(mbuf[rows, :], wd[...], preferred_element_type=F32)
 
-    steps = NZ // 2
-
-    def zstep(r, i):
+    def zsend(r, t):
         for d in (0, 1):
-            n = hops(d, r)
-            if i >= n:
+            if t > reaches(d, r):
                 continue
-            sign = 1 if d == 0 else -1
-            dest = lax.rem(z + NZ + sign * (n - i), NZ)
-            val = piece(r, dest)
-            if i > 0:
-                zcopy(d, r, i - 1).wait_recv()
-                val = val + rb[d, r, i - 1].astype(F32)
-            sb[d, r, i] = val.astype(BF16)
-            zcopy(d, r, i).start()
-        if i == steps:
-            val = piece(r, z)
-            for d in (0, 1):
-                end = hops(d, r) - 1
-                zcopy(d, r, end).wait_recv()
-                val = val + rb[d, r, end].astype(F32)
-            out[pl.ds(r * RB, RB), :] = val.astype(BF16)
+            val = piece(r, lax.rem(z + (t if d == 0 else NZ - t), NZ))
+            for u in ((), (2,), (3, 4), (), ())[t]:
+                if u <= reaches(d, r):
+                    zcopy(d, r, u).wait_recv()
+                    val = val + rb[d, r, u - 1].astype(F32)
+            sb[d, r, t - 1] = val.astype(BF16)
+            zcopy(d, r, t).start()
 
     for r in range(R):
         partial(r)
-        zstep(r, 0)
-    for i in range(1, steps + 1):
+        zsend(r, 4)
+        zsend(r, 3)
+    for t in (2, 1):
         for r in range(R):
-            zstep(r, i)
+            zsend(r, t)
+    for r in range(R):
+        val = piece(r, z)
+        for d in (0, 1):
+            zcopy(d, r, 1).wait_recv()
+            val = val + rb[d, r, 0].astype(F32)
+        out[pl.ds(r * RB, RB), :] = val.astype(BF16)
+
     for n, c in ((0, oc), (1, 0), (2, 1)):
         pltpu.make_async_copy(own_w, own_w, w_send.at[n]).wait()
 
@@ -396,16 +445,19 @@
         for c in (swap_k, swap_v, swap_q):
             c.wait_send()
 
-    for c in own_sends + [fwd_k, fwd_v] + list(core_sends.values()):
+    for c in own_sends[0] + own_sends[1]:
         c.wait_send()
+    for copies in passes.values():
+        for c in copies:
+            c.wait_send()
     for r in range(R):
         mcopy(r, 0).wait_send()
         mcopy(r, 1).wait_send()
         for h in range(4):
             pl.when(jnp.logical_and(core == r % 2, hslot != h))(mpass(h, r).wait_send)
         for d in (0, 1):
-            for i in range(hops(d, r)):
-                zcopy(d, r, i).wait_send()
+            for t in range(1, reaches(d, r) + 1):
+                zcopy(d, r, t).wait_send()
 
 
 def on_device(hidden, mask_flags, mask_embed, norm_gain, w_query, w_key, w_value, w_out):
@@ -440,7 +492,7 @@
             pltpu.VMEM((2, R, NZ // 2, RB, HD), BF16),
             dma((NKB,)), dma((NKB,)), dma((NKB,)), dma((5,)), dma((1,)),
             dma((3,)), dma((3,)), dma((3,)), dma((3,)),
-            dma((14,)), dma((2, 4, 2)), dma((2, R)), dma((4, R)), dma((4, R)),
+            dma((18,)), dma((2, 3, 2)), dma((2, 2, 2)), dma((2, R)), dma((4, R)), dma((4, R)),
             dma((2, R, NZ // 2)), dma((2, R, NZ // 2)),
         ],
         compiler_params=pltpu.CompilerParams(

time: 55.3 us -> 49.7 us (0.90); the launches traced: 55.2 us -> 49 us
  Pallas kernels: 53.6 us -> 47.4 us
    pallas_call x1, Pallas kernels: 53.6 us -> 47.4 us  [on_device(): pl.pallas_call(kernel, out_shape=jax.ShapeDtypeStruct((ROWS, HD), BF16),...]
where the time goes in v3:
time: 49.7 us; the launch traced here: 49 us
  Pallas kernels  47.4 us (95%)
  local copies, waits for them, and re-layouts  1.57 us (3%)
    pallas_call x1, Pallas kernels, on_device(): pl.pallas_call(kernel, out_shape=jax.ShapeDtypeStruct((ROWS, HD), BF16),...  47.4 us
    unnamed x1, local copies, waits for them, and re-layouts  1.57 us

profile of v3, /device:TPU:6, one launch (start us, length us, event | category | flops | bytes accessed | tf_op | source)
XLA Modules:
  0.0 49.0 jit_solution(5040825574775545931)
XLA Ops:
  0.0 47.4 %shard_map.91 = bf16[512,128]{1,0:T(8,128)(2,1)} custom-call(bf16[512,4096]{1,0:T(8,128)(2,1)} %hid.1, s32[4,128]{1,0:T(4,128)} %bitcast.3, bf16[4096]{0:T(1024)(128)(2,1)} %emb.1, f32[1,4096]{1,0:T(1,128)} %bitcast.2, bf16[4096,128]{1,0:T(8,128)(2,1)} %wq.1, bf16[4096,128]{1,0:T(8,128)(2,1)} %wk.1, bf16[4096,128]{1,0:T(8,128)(2,1)} %wv.1, ...), custom_call_target="tpu_custom_call" | custom-call | tf_op jit(solution)/shard_map/pallas_call | solution.py:466
  47.4 1.6 %copy.11 = bf16[512,128]{1,0:T(8,128)(2,1)} copy(bf16[512,128]{1,0:T(8,128)(2,1)} %shard_map.91) | data formatting | bytes 262144

commit v4 on v3

v4 whole, which is shorter than its diff:
```python
import math

import numpy as np
import jax
import jax.numpy as jnp
from jax import lax
from jax.sharding import PartitionSpec as P
from jax.experimental import pallas as pl
from jax.experimental.pallas import tpu as pltpu

D = 4096
HD = 128
SEQ = 4096
ROWS = 512
XROWS = 528
KB = 1024
NKB = D // KB
KQ = 512
R = 4
RB = ROWS // R
QB = 256
NZ = 8
NX = 4
MESH = pl.DeviceIdType.MESH
F32 = jnp.float32
BF16 = jnp.bfloat16


def rope_table():
    freqs = 500000.0 ** (-2.0 * np.arange(HD // 2) / HD)
    angles = np.arange(SEQ)[:, None] * freqs[None, :]
    return np.concatenate([np.cos(angles), np.sin(angles)], axis=1).astype(np.float32)


def kernel(hid, mask, emb, gain, wq, wk, wv, wo, tab, out,
           x, wkv_s, wq_s, emb_s, gain_s, mask_s, tab_s, maskc, ss, acc, qacc,
           kv, qs, m_s, o_s, pay, rx, acol, mbuf, wd, part, rb, sb,
           ld_x, ld_k, ld_v, ld_s, ld_w, w_send, w_recv, q_sem,
           kv_send, kv_recv, opp_recv, m_send, m_recv, p_send, p_recv, z_send, z_recv):
    ctx = lax.axis_index("ctx")
    tp = lax.axis_index("tp")
    xi, ylo = lax.rem(ctx, NX), lax.div(ctx, NX)
    yhi, z, core = lax.div(tp, 16), lax.rem(lax.div(tp, 2), NZ), lax.rem(tp, 2)

    def dev(x_=xi, ylo_=ylo, yhi_=yhi, z_=z, core_=core):
        return (ylo_ * NX + x_, yhi_ * 16 + z_ * 2 + core_)

    xr, xl = lax.rem(xi + 1, NX), lax.rem(xi + NX - 1, NX)
    xo = lax.rem(xi + 2, NX)
    zr, zl = lax.rem(z + 1, NZ), lax.rem(z + NZ - 1, NZ)
    zr2, zl2 = lax.rem(z + 2, NZ), lax.rem(z + NZ - 2, NZ)
    oc, oylo, oyhi = 1 - core, 1 - ylo, 1 - yhi

    c_gain = pltpu.make_async_copy(gain, gain_s, ld_s.at[0])
    c_emb = pltpu.make_async_copy(emb, emb_s, ld_s.at[1])
    c_mask = pltpu.make_async_copy(mask, mask_s, ld_s.at[2])
    c_tab = pltpu.make_async_copy(
        tab.at[pl.ds(pl.multiple_of(ctx * ROWS, ROWS), ROWS)], tab_s, ld_s.at[3])
    c_wq = pltpu.make_async_copy(wq, wq_s, ld_s.at[4])
    c_emb.start()
    c_gain.start()

    def xcopies(k):
        cols = pl.ds(pl.multiple_of(k * KB, KB), KB)
        return (
            pltpu.make_async_copy(hid.at[:, cols], x.at[pl.ds(0, ROWS), cols], ld_x.at[k]),
            pltpu.make_async_copy(wk.at[cols], wkv_s.at[cols, pl.ds(0, HD)], ld_k.at[k]),
            pltpu.make_async_copy(wv.at[cols], wkv_s.at[cols, pl.ds(HD, HD)], ld_v.at[k]),
        )

    def start_loads(k, _):
        for c in xcopies(k):
            c.start()
        return 0

    lax.fori_loop(0, NKB, start_loads, 0)
    c_mask.start()
    c_tab.start()
    c_wq.start()

    barrier = pltpu.get_barrier_semaphore()
    partners = [dev(x_=xr), dev(x_=xl), dev(z_=zr2), dev(z_=zl2), dev(z_=zr), dev(z_=zl), dev(core_=oc)]
    for c in (0, 1):
        partners += [dev(ylo_=oylo, core_=c), dev(yhi_=oyhi, core_=c),
                     dev(ylo_=oylo, yhi_=oyhi, core_=c)]
    for p in partners:
        pl.semaphore_signal(barrier, inc=1, device_id=p, device_id_type=MESH)

    my_rows = pl.ds(pl.multiple_of((yhi * 2 + core) * HD, HD), HD)

    def wsrc(half, zz, c):
        return wo.at[:, pl.ds(pl.multiple_of(half * 2048 + zz * 256 + c * HD, HD), HD)]

    def wdst(zz):
        return wd.at[zz, my_rows]

    def wcopies(zz):
        return (
            pltpu.make_async_copy(wsrc(yhi, zz, core), wdst(zz), ld_w.at[0]),
            pltpu.make_async_remote_copy(
                wsrc(yhi, zz, oc), wdst(zz), w_send.at[0], w_recv.at[0],
                device_id=dev(core_=oc), device_id_type=MESH),
            pltpu.make_async_remote_copy(
                wsrc(oyhi, zz, 0), wdst(zz), w_send.at[1], w_recv.at[1 + core],
                device_id=dev(ylo_=oylo, yhi_=oyhi, core_=0), device_id_type=MESH),
            pltpu.make_async_remote_copy(
                wsrc(oyhi, zz, 1), wdst(zz), w_send.at[2], w_recv.at[1 + core],
                device_id=dev(ylo_=oylo, yhi_=oyhi, core_=1), device_id_type=MESH),
        )

    def start_w(zz, _):
        for c in wcopies(zz):
            c.start()
        return 0

    c_emb.wait()
    c_gain.wait()
    x[pl.ds(ROWS, XROWS - ROWS), :] = jnp.broadcast_to(emb_s[...].reshape(1, D), (XROWS - ROWS, D))
    ss[...] = jnp.zeros_like(ss)
    acc[...] = jnp.zeros_like(acc)

    def kstep(k, _):
        for c in xcopies(k):
            c.wait()
        cols = pl.ds(pl.multiple_of(k * KB, KB), KB)
        xf = x[:, cols].astype(F32)
        sq = xf * xf
        total = sq[:, :128]
        for j in range(1, KB // 128):
            total = total + sq[:, j * 128:(j + 1) * 128]
        ss[...] += total
        xg = (xf * gain_s[:, cols]).astype(BF16)
        x[:, cols] = xg
        acc[...] += jnp.dot(xg, wkv_s[cols, :], preferred_element_type=F32)
        return 0

    lax.fori_loop(0, NKB, kstep, 0)
    c_mask.wait()
    c_tab.wait()
    scale = lax.rsqrt(jnp.sum(ss[...], axis=1, keepdims=True) * (1.0 / D) + 1e-05)
    ss[...] = jnp.broadcast_to(scale, (XROWS, 128))
    flags = (mask_s[...] == 1).astype(F32)
    for i in range(ROWS // 128):
        maskc[pl.ds(i * 128, 128), :] = jnp.transpose(
            jnp.broadcast_to(flags[i:i + 1, :], (128, 128)))

    def chosen(ref, lo):
        u = ref[:, lo:lo + HD] * ss[...]
        return jnp.where(maskc[...] > 0.5, u[ROWS:ROWS + 1, :], u[:ROWS, :])

    lane = lax.broadcasted_iota(jnp.int32, (ROWS, HD), 1)

    def rope(u):
        t = tab_s[...]
        r = pltpu.roll(t, HD // 2, 1)
        c = jnp.where(lane < HD // 2, t, r)
        s = jnp.where(lane < HD // 2, -r, t)
        return u * c + pltpu.roll(u, HD // 2, 1) * s

    kv[xi, 0] = rope(chosen(acc, 0)).astype(BF16)
    kv[xi, 1] = chosen(acc, HD).astype(BF16)

    pl.semaphore_wait(barrier, len(partners))

    OWN, LEFT, RIGHT, OPP = 0, 1, 2, 3
    slots = (xi, xl, xr, xo)
    to_r, to_l, to_c = dev(x_=xr), dev(x_=xl), dev(core_=oc)
    HALF = ROWS // 2

    def block(pos, w, half):
        if half is None:
            return kv.at[slots[pos], w]
        return kv.at[slots[pos], w, pl.ds(half * HALF, HALF)]

    def kvcopy(pos, w, half, n, recv, to):
        ref = block(pos, w, half)
        return pltpu.make_async_remote_copy(
            ref, ref, kv_send.at[n], recv, device_id=to, device_id_type=MESH)

    own_sends = []
    passes = {}
    for w in (0, 1):
        own_sends += [kvcopy(OWN, w, None, 2 * w, kv_recv.at[0, w], to_r),
                      kvcopy(OWN, w, None, 2 * w + 1, kv_recv.at[1, w], to_l)]
        passes[LEFT, w] = kvcopy(LEFT, w, 0, 4 + w, opp_recv.at[w, 0], to_r)
        passes[RIGHT, w] = kvcopy(RIGHT, w, 1, 6 + w, opp_recv.at[w, 1], to_l)

    def arrived(pos, w, h=None):
        ref = block(pos, w, h)
        sem = kv_recv.at[pos - LEFT, w] if h is None else opp_recv.at[w, h]
        pltpu.make_async_copy(ref, ref, sem).wait()

    for c in own_sends:
        c.start()

    lax.fori_loop(0, NZ, start_w, 0)

    c_wq.wait()
    qacc[...] = jnp.zeros_like(qacc)

    def qstep(k, _):
        cols = pl.ds(pl.multiple_of(k * KQ, KQ), KQ)
        qacc[...] += jnp.dot(x[:, cols], wq_s[cols, :], preferred_element_type=F32)
        return 0

    lax.fori_loop(0, D // KQ, qstep, 0)
    q_factor = math.log2(math.e) / math.sqrt(HD)
    qs[0] = (rope(chosen(qacc, 0)) * q_factor).astype(BF16)

    q_send = pltpu.make_async_remote_copy(
        qs.at[0], qs.at[1], q_sem.at[0], q_sem.at[1], device_id=dev(ylo_=oylo), device_id_type=MESH)
    q_send.start()

    ones = jnp.ones((ROWS, HD), BF16)

    def attend_rows(qset, pos, i):
        rows = pl.ds(i * QB, QB)
        slot = slots[pos]
        s = lax.dot_general(qs[qset, rows, :], kv[slot, 0], (((1,), (1,)), ((), ())),
                            preferred_element_type=F32)
        top = jnp.broadcast_to(jnp.max(s, axis=1, keepdims=True), (QB, HD))
        if pos != OWN:
            old = m_s[qset, rows, :]
            top = jnp.maximum(top, old)
        m_s[qset, rows, :] = top
        p = jnp.exp2(s - jnp.concatenate([top] * (ROWS // HD), axis=1)).astype(BF16)
        v = jnp.concatenate([kv[slot, 1], ones], axis=1)
        add = jnp.dot(p, v, preferred_element_type=F32)
        if pos == OWN:
            o_s[qset, rows, :] = add
        else:
            alpha = jnp.exp2(old - top)
            o_s[qset, rows, :] = o_s[qset, rows, :] * jnp.concatenate([alpha, alpha], axis=1) + add

    def attend(qset, pos):
        for i in range(ROWS // QB):
            attend_rows(qset, pos, i)

    attend(0, OWN)
    for w in (0, 1):
        for pos in (LEFT, RIGHT):
            arrived(pos, w)
            passes[pos, w].start()
    attend(0, LEFT)
    attend(0, RIGHT)
    q_send.wait_recv()
    attend(1, OWN)
    attend(1, LEFT)
    attend(1, RIGHT)
    for w in (0, 1):
        for h in (0, 1):
            arrived(OPP, w, h)

    myh = yhi * 2 + core
    HB = RB // 2
    piece_row = lax.broadcasted_iota(jnp.int32, (16, 128), 0)

    def mcopy(r, n, c):
        qset = (1, 1, 0)[n]
        to = (dev(ylo_=oylo, core_=c), dev(ylo_=oylo, yhi_=oyhi, core_=c), dev(yhi_=oyhi, core_=c))[n]
        return pltpu.make_async_remote_copy(
            pay.at[qset, r, c], rx.at[qset, myh, r], m_send.at[r, 2 * n + c],
            m_recv.at[qset, myh, r], device_id=to, device_id_type=MESH)

    def mbeside(r):
        return pltpu.make_async_remote_copy(
            pay.at[0, r, oc], rx.at[0, myh, r], m_send.at[r, 6],
            m_recv.at[0, myh, r], device_id=to_c, device_id_type=MESH)

    def pack(qset, r):
        rows = pl.ds(r * RB, RB)
        o = o_s[qset, rows, :]
        mix = (o[:, :HD] / o[:, HD:]).astype(BF16)
        lse = jnp.transpose(m_s[qset, rows, :] + jnp.log2(o[:, HD:]))[:16, :]
        hi = lse.astype(BF16).astype(F32)
        mid = (lse - hi).astype(BF16).astype(F32)
        low = lse - hi - mid
        stat = jnp.where(piece_row == 0, hi, jnp.where(piece_row == 1, mid, low)).astype(BF16)
        for c in (0, 1):
            pay[qset, r, c, pl.ds(0, HB), :] = mix[c * HB:(c + 1) * HB]
            pay[qset, r, c, pl.ds(HB, 16), :] = stat

    for i in range(ROWS // QB):
        attend_rows(1, OPP, i)
        attend_rows(0, OPP, i)
        for r in range(i * R * QB // ROWS, (i + 1) * R * QB // ROWS):
            pack(1, r)
            pack(0, r)
            for n in range(3):
                for c in (0, 1):
                    mcopy(r, n, c).start()
            mbeside(r).start()
            rx[0, myh, r] = pay[0, r, core]

    own_w = wd.at[:, my_rows]
    pltpu.make_async_copy(own_w, own_w, ld_w.at[0]).wait()
    for n, slot in ((0, yhi * 2 + oc), (1, oyhi * 2), (2, oyhi * 2 + 1)):
        ref = wd.at[:, pl.ds(pl.multiple_of(slot * HD, HD), HD)]
        pltpu.make_async_copy(ref, ref, w_recv.at[n]).wait()

    def reaches(d, r):
        return NZ // 2 if (d == 0) == (r < R // 2) else NZ // 2 - 1

    def zcopy(d, r, t):
        to = (zr2, zl2)[d] if t == 4 else (zr, zl)[d]
        return pltpu.make_async_remote_copy(
            sb.at[d, r, t - 1], rb.at[d, r, t - 1], z_send.at[d, r, t - 1], z_recv.at[d, r, t - 1],
            device_id=dev(z_=to), device_id_type=MESH)

    def piece(r, dest):
        return part[dest, pl.ds(r * RB, RB)]

    def mhalf(r, c):
        return mbuf.at[pl.ds(pl.multiple_of(r * RB + c * HB, HB), HB)]

    def mpass(r):
        return pltpu.make_async_remote_copy(
            mhalf(r, core), mhalf(r, core), p_send.at[r], p_recv.at[r],
            device_id=to_c, device_id_type=MESH)

    def take(r):
        for k in range(4):
            h = lax.rem(myh + k, 4)
            for n in (0, 1) if k else (1,):
                ref = rx.at[n, h, r]
                pltpu.make_async_copy(ref, ref, m_recv.at[n, h, r]).wait()
        for h in range(4):
            logs = []
            for n in (0, 1):
                t = rx[n, h, r, pl.ds(HB, 16), :].astype(F32)
                logs.append(t[0:1] + t[1:2] + t[2:3])
            share = 1.0 / (1.0 + jnp.exp2(logs[1] - logs[0]))
            acol[h] = jnp.transpose(jnp.broadcast_to(share, (128, 128)))
        rows = pl.ds(pl.multiple_of(r * RB + core * HB, HB), HB)
        for h in range(4):
            a = acol[h, pl.ds(pl.multiple_of(core * HB, HB), HB), :]
            u = rx[0, h, r, pl.ds(0, HB), :].astype(F32)
            v = rx[1, h, r, pl.ds(0, HB), :].astype(F32)
            mbuf[rows, pl.ds(h * HD, HD)] = (u * a + v * (1.0 - a)).astype(BF16)
        mpass(r).start()

    def taken(r):
        pltpu.make_async_copy(mhalf(r, oc), mhalf(r, oc), p_recv.at[r]).wait()

    def partial(rows, a, b):
        a, b = lax.rem(z + NZ + a, NZ), lax.rem(z + NZ + b, NZ)
        both = jnp.dot(mbuf[rows, :], jnp.concatenate([wd[a], wd[b]], axis=1),
                       preferred_element_type=F32)
        part[a, rows] = both[:, :HD]
        part[b, rows] = both[:, HD:]

    def zsend(r, t):
        for d in (0, 1):
            if t > reaches(d, r):
                continue
            val = piece(r, lax.rem(z + (t if d == 0 else NZ - t), NZ))
            for u in ((), (2,), (3, 4), (), ())[t]:
                if u <= reaches(d, r):
                    zcopy(d, r, u).wait_recv()
                    val = val + rb[d, r, u - 1].astype(F32)
            sb[d, r, t - 1] = val.astype(BF16)
            zcopy(d, r, t).start()

    take(0)
    for r in range(R):
        if r + 1 < R:
            take(r + 1)
        taken(r)
        rows = pl.ds(r * RB, RB)
        partial(rows, 4, 3)
        partial(rows, -3, -2)
        zsend(r, 4)
        zsend(r, 3)
    partial(pl.ds(0, ROWS), 2, 1)
    partial(pl.ds(0, ROWS), -1, 0)
    for t in (2, 1):
        for r in range(R):
            zsend(r, t)
    for r in range(R):
        val = piece(r, z)
        for d in (0, 1):
            zcopy(d, r, 1).wait_recv()
            val = val + rb[d, r, 0].astype(F32)
        out[pl.ds(r * RB, RB), :] = val.astype(BF16)

    for n, c in ((0, oc), (1, 0), (2, 1)):
        pltpu.make_async_copy(own_w, own_w, w_send.at[n]).wait()

    q_send.wait_send()
    for c in own_sends + list(passes.values()):
        c.wait_send()
    for r in range(R):
        for n in range(3):
            for c in (0, 1):
                mcopy(r, n, c).wait_send()
        mbeside(r).wait_send()
        mpass(r).wait_send()
        for d in (0, 1):
            for t in range(1, reaches(d, r) + 1):
                zcopy(d, r, t).wait_send()


def on_device(hidden, mask_flags, mask_embed, norm_gain, w_query, w_key, w_value, w_out):
    any_spec = pl.BlockSpec(memory_space=pl.ANY)
    dma = pltpu.SemaphoreType.DMA
    return pl.pallas_call(
        kernel,
        out_shape=jax.ShapeDtypeStruct((ROWS, HD), BF16),
        in_specs=[any_spec] * 9,
        out_specs=pl.BlockSpec(memory_space=pltpu.VMEM),
        scratch_shapes=[
            pltpu.VMEM((XROWS, D), BF16),
            pltpu.VMEM((D, 2 * HD), BF16),
            pltpu.VMEM((D, HD), BF16),
            pltpu.VMEM((D,), BF16),
            pltpu.VMEM((1, D), F32),
            pltpu.VMEM((ROWS // 128, 128), jnp.int32),
            pltpu.VMEM((ROWS, HD), F32),
            pltpu.VMEM((ROWS, 128), F32),
            pltpu.VMEM((XROWS, 128), F32),
            pltpu.VMEM((XROWS, 2 * HD), F32),
            pltpu.VMEM((XROWS, HD), F32),
            pltpu.VMEM((NX, 2, ROWS, HD), BF16),
            pltpu.VMEM((2, ROWS, HD), BF16),
            pltpu.VMEM((2, ROWS, HD), F32),
            pltpu.VMEM((2, ROWS, 2 * HD), F32),
            pltpu.VMEM((2, R, 2, RB // 2 + 16, HD), BF16),
            pltpu.VMEM((2, 4, R, RB // 2 + 16, HD), BF16),
            pltpu.VMEM((4, 128, 128), F32),
            pltpu.VMEM((ROWS, 4 * HD), BF16),
            pltpu.VMEM((NZ, 4 * HD, HD), BF16),
            pltpu.VMEM((NZ, ROWS, HD), F32),
            pltpu.VMEM((2, R, NZ // 2, RB, HD), BF16),
            pltpu.VMEM((2, R, NZ // 2, RB, HD), BF16),
            dma((NKB,)), dma((NKB,)), dma((NKB,)), dma((5,)), dma((1,)),
            dma((3,)), dma((3,)), dma((2,)),
            dma((8,)), dma((2, 2)), dma((2, 2)), dma((R, 7)), dma((2, 4, R)), dma((R,)), dma((R,)),
            dma((2, R, NZ // 2)), dma((2, R, NZ // 2)),
        ],
        compiler_params=pltpu.CompilerParams(
            collective_id=0, has_side_effects=True, vmem_limit_bytes=62 * 1024 * 1024),
    )(hidden, mask_flags.reshape(ROWS // 128, 128), mask_embed,
      norm_gain.reshape(1, D), w_query, w_key, w_value, w_out, jnp.asarray(rope_table()))


def solution(mesh):
    in_specs = (
        P("ctx", None),
        P("ctx"),
        P(),
        P(),
        P(None, "tp"),
        P(None, "tp"),
        P(None, "tp"),
        P("tp", None),
    )
    return jax.shard_map(
        on_device, mesh=mesh, in_specs=in_specs, out_specs=P("ctx", "tp"), check_vma=False
    )
```

time: 49.7 us -> 48.5 us (0.976)
  Pallas kernels: 47.4 us -> 46.4 us
    pallas_call x1, Pallas kernels: 47.4 us -> 46.4 us  [on_device(): pl.pallas_call(kernel, out_shape=jax.ShapeDtypeStruct((ROWS, HD), BF16),...]
where the time goes in v4:
time: 48.5 us; the launch traced here: 48 us
  Pallas kernels  46.4 us (96%)
  local copies, waits for them, and re-layouts  1.57 us (3%)
    pallas_call x1, Pallas kernels, on_device(): pl.pallas_call(kernel, out_shape=jax.ShapeDtypeStruct((ROWS, HD), BF16),...  46.4 us
    unnamed x1, local copies, waits for them, and re-layouts  1.57 us

profile of v4, /device:TPU:6, one launch (start us, length us, event | category | flops | bytes accessed | tf_op | source)
XLA Modules:
  0.0 48.0 jit_solution(1376627373701747065)
XLA Ops:
  0.0 46.4 %shard_map.91 = bf16[512,128]{1,0:T(8,128)(2,1)} custom-call(bf16[512,4096]{1,0:T(8,128)(2,1)} %hid.1, s32[4,128]{1,0:T(4,128)} %bitcast.3, bf16[4096]{0:T(1024)(128)(2,1)} %emb.1, f32[1,4096]{1,0:T(1,128)} %bitcast.2, bf16[4096,128]{1,0:T(8,128)(2,1)} %wq.1, bf16[4096,128]{1,0:T(8,128)(2,1)} %wk.1, bf16[4096,128]{1,0:T(8,128)(2,1)} %wv.1, ...), custom_call_target="tpu_custom_call" | custom-call | tf_op jit(solution)/shard_map/pallas_call | solution.py:406
  46.4 1.6 %copy.11 = bf16[512,128]{1,0:T(8,128)(2,1)} copy(bf16[512,128]{1,0:T(8,128)(2,1)} %shard_map.91) | data formatting | bytes 262144

commit v5 on v4

--- a/solution.py
+++ b/solution.py
@@ -34,7 +34,7 @@
 
 def kernel(hid, mask, emb, gain, wq, wk, wv, wo, tab, out,
            x, wkv_s, wq_s, emb_s, gain_s, mask_s, tab_s, maskc, ss, acc, qacc,
-           kv, qs, m_s, o_s, pay, rx, acol, mbuf, wd, part, rb, sb,
+           kv, qs, m_s, o_s, pay, rx, mbuf, wd, part, rb, sb,
            ld_x, ld_k, ld_v, ld_s, ld_w, w_send, w_recv, q_sem,
            kv_send, kv_recv, opp_recv, m_send, m_recv, p_send, p_recv, z_send, z_recv):
     ctx = lax.axis_index("ctx")
@@ -213,12 +213,12 @@
 
     ones = jnp.ones((ROWS, HD), BF16)
 
-    def attend_rows(qset, pos, i):
-        rows = pl.ds(i * QB, QB)
+    def attend_rows(qset, pos, i, n=QB):
+        rows = pl.ds(i * n, n)
         slot = slots[pos]
         s = lax.dot_general(qs[qset, rows, :], kv[slot, 0], (((1,), (1,)), ((), ())),
                             preferred_element_type=F32)
-        top = jnp.broadcast_to(jnp.max(s, axis=1, keepdims=True), (QB, HD))
+        top = jnp.broadcast_to(jnp.max(s, axis=1, keepdims=True), (n, HD))
         if pos != OWN:
             old = m_s[qset, rows, :]
             top = jnp.maximum(top, old)
@@ -252,45 +252,43 @@
             arrived(OPP, w, h)
 
     myh = yhi * 2 + core
-    HB = RB // 2
     piece_row = lax.broadcasted_iota(jnp.int32, (16, 128), 0)
 
-    def mcopy(r, n, c):
-        qset = (1, 1, 0)[n]
-        to = (dev(ylo_=oylo, core_=c), dev(ylo_=oylo, yhi_=oyhi, core_=c), dev(yhi_=oyhi, core_=c))[n]
+    def mcopy(r, n):
+        qset = (1, 1, 0, 0)[n]
+        c = r % 2
+        to = (dev(ylo_=oylo, core_=c), dev(ylo_=oylo, yhi_=oyhi, core_=c), dev(yhi_=oyhi, core_=c), to_c)[n]
         return pltpu.make_async_remote_copy(
-            pay.at[qset, r, c], rx.at[qset, myh, r], m_send.at[r, 2 * n + c],
+            pay.at[qset, r], rx.at[qset, myh, r], m_send.at[r, n],
             m_recv.at[qset, myh, r], device_id=to, device_id_type=MESH)
-
-    def mbeside(r):
-        return pltpu.make_async_remote_copy(
-            pay.at[0, r, oc], rx.at[0, myh, r], m_send.at[r, 6],
-            m_recv.at[0, myh, r], device_id=to_c, device_id_type=MESH)
 
     def pack(qset, r):
         rows = pl.ds(r * RB, RB)
         o = o_s[qset, rows, :]
-        mix = (o[:, :HD] / o[:, HD:]).astype(BF16)
         lse = jnp.transpose(m_s[qset, rows, :] + jnp.log2(o[:, HD:]))[:16, :]
         hi = lse.astype(BF16).astype(F32)
         mid = (lse - hi).astype(BF16).astype(F32)
         low = lse - hi - mid
-        stat = jnp.where(piece_row == 0, hi, jnp.where(piece_row == 1, mid, low)).astype(BF16)
-        for c in (0, 1):
-            pay[qset, r, c, pl.ds(0, HB), :] = mix[c * HB:(c + 1) * HB]
-            pay[qset, r, c, pl.ds(HB, 16), :] = stat
-
-    for i in range(ROWS // QB):
-        attend_rows(1, OPP, i)
-        attend_rows(0, OPP, i)
-        for r in range(i * R * QB // ROWS, (i + 1) * R * QB // ROWS):
-            pack(1, r)
-            pack(0, r)
-            for n in range(3):
-                for c in (0, 1):
-                    mcopy(r, n, c).start()
-            mbeside(r).start()
-            rx[0, myh, r] = pay[0, r, core]
+        stat = jnp.where(piece_row == 0, hi, jnp.where(piece_row == 1, mid, low))
+        pay[qset, r, pl.ds(0, RB), :] = (o[:, :HD] / o[:, HD:]).astype(BF16)
+        pay[qset, r, pl.ds(RB, 16), :] = stat.astype(BF16)
+
+    for r in range(R):
+        attend_rows(1, OPP, r, RB)
+        pack(1, r)
+        mcopy(r, 0).start()
+        mcopy(r, 1).start()
+        attend_rows(0, OPP, r, RB)
+        pack(0, r)
+        mcopy(r, 2).start()
+
+        @pl.when(core == r % 2)
+        def _():
+            rx[0, myh, r] = pay[0, r]
+
+        @pl.when(core != r % 2)
+        def _():
+            mcopy(r, 3).start()
 
     own_w = wd.at[:, my_rows]
     pltpu.make_async_copy(own_w, own_w, ld_w.at[0]).wait()
@@ -299,7 +297,7 @@
         pltpu.make_async_copy(ref, ref, w_recv.at[n]).wait()
 
     def reaches(d, r):
-        return NZ // 2 if (d == 0) == (r < R // 2) else NZ // 2 - 1
+        return NZ // 2 if (d == 0) == (r % 2 == 0) else NZ // 2 - 1
 
     def zcopy(d, r, t):
         to = (zr2, zl2)[d] if t == 4 else (zr, zl)[d]
@@ -310,13 +308,10 @@
     def piece(r, dest):
         return part[dest, pl.ds(r * RB, RB)]
 
-    def mhalf(r, c):
-        return mbuf.at[pl.ds(pl.multiple_of(r * RB + c * HB, HB), HB)]
-
     def mpass(r):
+        ref = mbuf.at[pl.ds(r * RB, RB)]
         return pltpu.make_async_remote_copy(
-            mhalf(r, core), mhalf(r, core), p_send.at[r], p_recv.at[r],
-            device_id=to_c, device_id_type=MESH)
+            ref, ref, p_send.at[r], p_recv.at[r], device_id=to_c, device_id_type=MESH)
 
     def take(r):
         for k in range(4):
@@ -327,20 +322,14 @@
         for h in range(4):
             logs = []
             for n in (0, 1):
-                t = rx[n, h, r, pl.ds(HB, 16), :].astype(F32)
+                t = rx[n, h, r, pl.ds(RB, 16), :].astype(F32)
                 logs.append(t[0:1] + t[1:2] + t[2:3])
             share = 1.0 / (1.0 + jnp.exp2(logs[1] - logs[0]))
-            acol[h] = jnp.transpose(jnp.broadcast_to(share, (128, 128)))
-        rows = pl.ds(pl.multiple_of(r * RB + core * HB, HB), HB)
-        for h in range(4):
-            a = acol[h, pl.ds(pl.multiple_of(core * HB, HB), HB), :]
-            u = rx[0, h, r, pl.ds(0, HB), :].astype(F32)
-            v = rx[1, h, r, pl.ds(0, HB), :].astype(F32)
-            mbuf[rows, pl.ds(h * HD, HD)] = (u * a + v * (1.0 - a)).astype(BF16)
+            a = jnp.transpose(jnp.broadcast_to(share, (RB, HD)))
+            u = rx[0, h, r, pl.ds(0, RB), :].astype(F32)
+            v = rx[1, h, r, pl.ds(0, RB), :].astype(F32)
+            mbuf[pl.ds(r * RB, RB), pl.ds(h * HD, HD)] = (u * a + v * (1.0 - a)).astype(BF16)
         mpass(r).start()
-
-    def taken(r):
-        pltpu.make_async_copy(mhalf(r, oc), mhalf(r, oc), p_recv.at[r]).wait()
 
     def partial(rows, a, b):
         a, b = lax.rem(z + NZ + a, NZ), lax.rem(z + NZ + b, NZ)
@@ -361,11 +350,12 @@
             sb[d, r, t - 1] = val.astype(BF16)
             zcopy(d, r, t).start()
 
-    take(0)
     for r in range(R):
-        if r + 1 < R:
-            take(r + 1)
-        taken(r)
+        @pl.when(core == r % 2)
+        def _():
+            take(r)
+
+        pl.when(core != r % 2)(mpass(r).wait_recv)
         rows = pl.ds(r * RB, RB)
         partial(rows, 4, 3)
         partial(rows, -3, -2)
@@ -391,10 +381,9 @@
         c.wait_send()
     for r in range(R):
         for n in range(3):
-            for c in (0, 1):
-                mcopy(r, n, c).wait_send()
-        mbeside(r).wait_send()
-        mpass(r).wait_send()
+            mcopy(r, n).wait_send()
+        pl.when(core != r % 2)(mcopy(r, 3).wait_send)
+        pl.when(core == r % 2)(mpass(r).wait_send)
         for d in (0, 1):
             for t in range(1, reaches(d, r) + 1):
                 zcopy(d, r, t).wait_send()
@@ -424,9 +413,8 @@
             pltpu.VMEM((2, ROWS, HD), BF16),
             pltpu.VMEM((2, ROWS, HD), F32),
             pltpu.VMEM((2, ROWS, 2 * HD), F32),
-            pltpu.VMEM((2, R, 2, RB // 2 + 16, HD), BF16),
-            pltpu.VMEM((2, 4, R, RB // 2 + 16, HD), BF16),
-            pltpu.VMEM((4, 128, 128), F32),
+            pltpu.VMEM((2, R, RB + 16, HD), BF16),
+            pltpu.VMEM((2, 4, R, RB + 16, HD), BF16),
             pltpu.VMEM((ROWS, 4 * HD), BF16),
             pltpu.VMEM((NZ, 4 * HD, HD), BF16),
             pltpu.VMEM((NZ, ROWS, HD), F32),
@@ -434,7 +422,7 @@
             pltpu.VMEM((2, R, NZ // 2, RB, HD), BF16),
             dma((NKB,)), dma((NKB,)), dma((NKB,)), dma((5,)), dma((1,)),
             dma((3,)), dma((3,)), dma((2,)),
-            dma((8,)), dma((2, 2)), dma((2, 2)), dma((R, 7)), dma((2, 4, R)), dma((R,)), dma((R,)),
+            dma((8,)), dma((2, 2)), dma((2, 2)), dma((R, 4)), dma((2, 4, R)), dma((R,)), dma((R,)),
             dma((2, R, NZ // 2)), dma((2, R, NZ // 2)),
         ],
         compiler_params=pltpu.CompilerParams(

time: 48.5 us -> 48.1 us (level)
  no operation moved by 1% of the time
where the time goes in v5:
time: 48.1 us; the launch traced here: 47.9 us
  Pallas kernels  46.4 us (96%)
  local copies, waits for them, and re-layouts  1.57 us (3%)
    pallas_call x1, Pallas kernels, on_device(): pl.pallas_call(kernel, out_shape=jax.ShapeDtypeStruct((ROWS, HD), BF16),...  46.4 us
    unnamed x1, local copies, waits for them, and re-layouts  1.57 us

profile of v5, /device:TPU:6, one launch (start us, length us, event | category | flops | bytes accessed | tf_op | source)
XLA Modules:
  0.0 47.9 jit_solution(8194236107741516654)
XLA Ops:
  0.0 46.4 %shard_map.91 = bf16[512,128]{1,0:T(8,128)(2,1)} custom-call(bf16[512,4096]{1,0:T(8,128)(2,1)} %hid.1, s32[4,128]{1,0:T(4,128)} %bitcast.3, bf16[4096]{0:T(1024)(128)(2,1)} %emb.1, f32[1,4096]{1,0:T(1,128)} %bitcast.2, bf16[4096,128]{1,0:T(8,128)(2,1)} %wq.1, bf16[4096,128]{1,0:T(8,128)(2,1)} %wk.1, bf16[4096,128]{1,0:T(8,128)(2,1)} %wv.1, ...), custom_call_target="tpu_custom_call" | custom-call | tf_op jit(solution)/shard_map/pallas_call | solution.py:395
  46.4 1.6 %copy.11 = bf16[512,128]{1,0:T(8,128)(2,1)} copy(bf16[512,128]{1,0:T(8,128)(2,1)} %shard_map.91) | data formatting | bytes 262144

commit v6 on v5

--- a/solution.py
+++ b/solution.py
@@ -88,30 +88,24 @@
 
     my_rows = pl.ds(pl.multiple_of((yhi * 2 + core) * HD, HD), HD)
 
-    def wsrc(half, zz, c):
+    def wsrc(half, j, c):
+        zz = lax.rem(z + 3 + j, NZ)
         return wo.at[:, pl.ds(pl.multiple_of(half * 2048 + zz * 256 + c * HD, HD), HD)]
 
-    def wdst(zz):
-        return wd.at[zz, my_rows]
-
     def wcopies(zz):
+        g = zz // 4
         return (
-            pltpu.make_async_copy(wsrc(yhi, zz, core), wdst(zz), ld_w.at[0]),
+            pltpu.make_async_copy(wsrc(yhi, zz, core), wd.at[zz, my_rows], ld_w.at[g]),
             pltpu.make_async_remote_copy(
-                wsrc(yhi, zz, oc), wdst(zz), w_send.at[0], w_recv.at[0],
+                wsrc(yhi, zz, oc), wd.at[zz, my_rows], w_send.at[0], w_recv.at[g, 0],
                 device_id=dev(core_=oc), device_id_type=MESH),
             pltpu.make_async_remote_copy(
-                wsrc(oyhi, zz, 0), wdst(zz), w_send.at[1], w_recv.at[1 + core],
+                wsrc(oyhi, zz, 0), wd.at[zz, my_rows], w_send.at[1], w_recv.at[g, 1 + core],
                 device_id=dev(ylo_=oylo, yhi_=oyhi, core_=0), device_id_type=MESH),
             pltpu.make_async_remote_copy(
-                wsrc(oyhi, zz, 1), wdst(zz), w_send.at[2], w_recv.at[1 + core],
+                wsrc(oyhi, zz, 1), wd.at[zz, my_rows], w_send.at[2], w_recv.at[g, 1 + core],
                 device_id=dev(ylo_=oylo, yhi_=oyhi, core_=1), device_id_type=MESH),
         )
-
-    def start_w(zz, _):
-        for c in wcopies(zz):
-            c.start()
-        return 0
 
     c_emb.wait()
     c_gain.wait()
@@ -193,7 +187,9 @@
     for c in own_sends:
         c.start()
 
-    lax.fori_loop(0, NZ, start_w, 0)
+    for j in range(NZ):
+        for c in wcopies(j):
+            c.start()
 
     c_wq.wait()
     qacc[...] = jnp.zeros_like(qacc)
@@ -291,10 +287,14 @@
             mcopy(r, 3).start()
 
     own_w = wd.at[:, my_rows]
-    pltpu.make_async_copy(own_w, own_w, ld_w.at[0]).wait()
-    for n, slot in ((0, yhi * 2 + oc), (1, oyhi * 2), (2, oyhi * 2 + 1)):
-        ref = wd.at[:, pl.ds(pl.multiple_of(slot * HD, HD), HD)]
-        pltpu.make_async_copy(ref, ref, w_recv.at[n]).wait()
+
+    def w_here(g):
+        for n, slot in ((None, yhi * 2 + core), (0, yhi * 2 + oc), (1, oyhi * 2), (2, oyhi * 2 + 1)):
+            ref = wd.at[pl.ds(4 * g, 4), pl.ds(pl.multiple_of(slot * HD, HD), HD)]
+            sem = ld_w.at[g] if n is None else w_recv.at[g, n]
+            pltpu.make_async_copy(ref, ref, sem).wait()
+
+    w_here(0)
 
     def reaches(d, r):
         return NZ // 2 if (d == 0) == (r % 2 == 0) else NZ // 2 - 1
@@ -305,8 +305,8 @@
             sb.at[d, r, t - 1], rb.at[d, r, t - 1], z_send.at[d, r, t - 1], z_recv.at[d, r, t - 1],
             device_id=dev(z_=to), device_id_type=MESH)
 
-    def piece(r, dest):
-        return part[dest, pl.ds(r * RB, RB)]
+    def piece(r, ahead):
+        return part[(ahead - 3) % NZ, pl.ds(r * RB, RB)]
 
     def mpass(r):
         ref = mbuf.at[pl.ds(r * RB, RB)]
@@ -332,7 +332,7 @@
         mpass(r).start()
 
     def partial(rows, a, b):
-        a, b = lax.rem(z + NZ + a, NZ), lax.rem(z + NZ + b, NZ)
+        a, b = (a - 3) % NZ, (b - 3) % NZ
         both = jnp.dot(mbuf[rows, :], jnp.concatenate([wd[a], wd[b]], axis=1),
                        preferred_element_type=F32)
         part[a, rows] = both[:, :HD]
@@ -342,7 +342,7 @@
         for d in (0, 1):
             if t > reaches(d, r):
                 continue
-            val = piece(r, lax.rem(z + (t if d == 0 else NZ - t), NZ))
+            val = piece(r, t if d == 0 else -t)
             for u in ((), (2,), (3, 4), (), ())[t]:
                 if u <= reaches(d, r):
                     zcopy(d, r, u).wait_recv()
@@ -351,23 +351,29 @@
             zcopy(d, r, t).start()
 
     for r in range(R):
-        @pl.when(core == r % 2)
+        if r == 0:
+            @pl.when(core == 0)
+            def _():
+                take(0)
+
+        @pl.when(core != r % 2)
         def _():
-            take(r)
-
-        pl.when(core != r % 2)(mpass(r).wait_recv)
+            if r + 1 < R:
+                take(r + 1)
+            mpass(r).wait_recv()
         rows = pl.ds(r * RB, RB)
         partial(rows, 4, 3)
         partial(rows, -3, -2)
         zsend(r, 4)
         zsend(r, 3)
+    w_here(1)
     partial(pl.ds(0, ROWS), 2, 1)
     partial(pl.ds(0, ROWS), -1, 0)
     for t in (2, 1):
         for r in range(R):
             zsend(r, t)
     for r in range(R):
-        val = piece(r, z)
+        val = piece(r, 0)
         for d in (0, 1):
             zcopy(d, r, 1).wait_recv()
             val = val + rb[d, r, 0].astype(F32)
@@ -420,8 +426,8 @@
             pltpu.VMEM((NZ, ROWS, HD), F32),
             pltpu.VMEM((2, R, NZ // 2, RB, HD), BF16),
             pltpu.VMEM((2, R, NZ // 2, RB, HD), BF16),
-            dma((NKB,)), dma((NKB,)), dma((NKB,)), dma((5,)), dma((1,)),
-            dma((3,)), dma((3,)), dma((2,)),
+            dma((NKB,)), dma((NKB,)), dma((NKB,)), dma((5,)), dma((2,)),
+            dma((3,)), dma((2, 3)), dma((2,)),
             dma((8,)), dma((2, 2)), dma((2, 2)), dma((R, 4)), dma((2, 4, R)), dma((R,)), dma((R,)),
             dma((2, R, NZ // 2)), dma((2, R, NZ // 2)),
         ],

time: 48.1 us -> 47.1 us (0.979)
  Pallas kernels: 46.4 us -> 45.3 us
    pallas_call x1, Pallas kernels: 46.4 us -> 45.3 us  [on_device(): pl.pallas_call(kernel, out_shape=jax.ShapeDtypeStruct((ROWS, HD), BF16),...]
where the time goes in v6:
time: 47.1 us; the launch traced here: 46.9 us
  Pallas kernels  45.3 us (96%)
  local copies, waits for them, and re-layouts  1.57 us (3%)
    pallas_call x1, Pallas kernels, on_device(): pl.pallas_call(kernel, out_shape=jax.ShapeDtypeStruct((ROWS, HD), BF16),...  45.3 us
    unnamed x1, local copies, waits for them, and re-layouts  1.57 us

profile of v6, /device:TPU:6, one launch (start us, length us, event | category | flops | bytes accessed | tf_op | source)
XLA Modules:
  0.0 46.9 jit_solution(8590105907728822265)
XLA Ops:
  0.0 45.3 %shard_map.91 = bf16[512,128]{1,0:T(8,128)(2,1)} custom-call(bf16[512,4096]{1,0:T(8,128)(2,1)} %hid.1, s32[4,128]{1,0:T(4,128)} %bitcast.3, bf16[4096]{0:T(1024)(128)(2,1)} %emb.1, f32[1,4096]{1,0:T(1,128)} %bitcast.2, bf16[4096,128]{1,0:T(8,128)(2,1)} %wq.1, bf16[4096,128]{1,0:T(8,128)(2,1)} %wk.1, bf16[4096,128]{1,0:T(8,128)(2,1)} %wv.1, ...), custom_call_target="tpu_custom_call" | custom-call | tf_op jit(solution)/shard_map/pallas_call | solution.py:401
  45.3 1.6 %copy.11 = bf16[512,128]{1,0:T(8,128)(2,1)} copy(bf16[512,128]{1,0:T(8,128)(2,1)} %shard_map.91) | data formatting | bytes 262144
